TPU v7x, 256 devices: a whole 4x4x8 slice. The times are simulated.
256 devices in a mesh: seq: 256 (over y, x, z, core).
Axes of the slice: x: 4, y: 4, z: 8, core: 2. Of those that a mesh axis runs over, the one named last changes fastest.
Arguments:
- query_rows: bfloat16 [65536, 1024], P('seq'), may hold values from -64 to 64
- key_rows: bfloat16 [65536, 1024], P('seq'), may hold values from -64 to 64
- value_rows: bfloat16 [65536, 1024], P('seq'), may hold values from -8 to 8
- out_grad: bfloat16 [65536, 1024], P('seq'), may hold values from -6 to 6
Outputs:
- attended: bfloat16 [65536, 1024], P('seq')
- query_grad: bfloat16 [65536, 1024], P('seq')
- key_grad: bfloat16 [65536, 1024], P('seq')
- value_grad: bfloat16 [65536, 1024], P('seq')
All inputs are finite; a program needn't handle non-finite values.
Results may differ from a plain program's by a relative error of at most 0.022.
Values may be sent and summed in bfloat16 or wider, within the bound.
No kernel may reach another device: no remote copies, remote signals or barrier semaphores. Data moves between devices by JAX's collectives and lax.ppermute only.
A program may use at most 128 MiB of HBM per device.

v0:
```python
import functools
import math

import jax
import jax.numpy as jnp
from jax import lax
from jax.experimental import pallas as pl
from jax.experimental.pallas import tpu as pltpu
from jax.sharding import PartitionSpec as P

H = 16
E = 64
B = 128
LANES = 128
PAIRS = 8
RING = 16
LN2 = math.log(2.0)
F32 = jnp.float32
BF16 = jnp.bfloat16

ROWS = {l: 1024 >> (l - 2) for l in range(3, 9)}
FIRST = {3: 0, 4: 512, 5: 768, 6: 896, 7: 960, 8: 992}
STACK = 1024


def dot(a, b):
    return lax.dot_general(a, b, (((1,), (0,)), ((), ())), preferred_element_type=F32)


def dot_nt(a, b):
    return lax.dot_general(a, b, (((1,), (1,)), ((), ())), preferred_element_type=F32)


def dot_tn(a, b):
    return lax.dot_general(a, b, (((0,), (0,)), ((), ())), preferred_element_type=F32)


def lane_of(rows):
    return lax.broadcasted_iota(jnp.int32, (rows, LANES), 1)


def low_lanes(rows):
    return lane_of(rows) < E


def swap_halves(x):
    return pltpu.roll(x, E, 1)


def shift_of(factor):
    return factor.bit_length() - 1


def pool_matrix(rows_out, factor=2):
    r = lax.broadcasted_iota(jnp.int32, (rows_out, rows_out * factor), 0)
    c = lax.broadcasted_iota(jnp.int32, (rows_out, rows_out * factor), 1)
    return jnp.where(c >> shift_of(factor) == r, 1.0 / factor, 0.0).astype(BF16)


def spread_matrix(rows_in, factor, value=1.0):
    r = lax.broadcasted_iota(jnp.int32, (rows_in * factor, rows_in), 0)
    c = lax.broadcasted_iota(jnp.int32, (rows_in * factor, rows_in), 1)
    return jnp.where(r >> shift_of(factor) == c, value, 0.0).astype(BF16)


def pieces(x, count):
    out = []
    for _ in range(count):
        part = x.astype(BF16)
        out.append(part)
        x = x - part.astype(F32)
    return out


def spread(matrix, x, count):
    total = None
    for part in pieces(x, count):
        term = dot(matrix, part)
        total = term if total is None else total + term
    return total


def halved(scratch, x):
    rows = x.shape[0]
    scratch[0:rows, :] = x
    first = scratch[pl.ds(0, rows // 2, stride=2), :]
    second = scratch[pl.ds(1, rows // 2, stride=2), :]
    return ((first + second) * 0.5).astype(BF16)


def repeated(scratch, x, factor):
    rows = x.shape[0]
    for i in range(factor):
        scratch[pl.ds(i, rows, stride=factor), :] = x
    return scratch[0 : rows * factor, :]


def call(kernel, outs, ins, scratch=(), flops=1e8, smem_first=False):
    specs = [pl.BlockSpec(memory_space=pltpu.VMEM) for _ in ins]
    if smem_first:
        specs[0] = pl.BlockSpec(memory_space=pltpu.SMEM)
    return pl.pallas_call(
        kernel,
        out_shape=[jax.ShapeDtypeStruct(s, d) for s, d in outs],
        in_specs=specs,
        out_specs=[pl.BlockSpec(memory_space=pltpu.VMEM) for _ in outs],
        scratch_shapes=list(scratch),
        compiler_params=pltpu.CompilerParams(vmem_limit_bytes=40 * 1024 * 1024),
        cost_estimate=pl.CostEstimate(
            flops=int(flops), bytes_accessed=2_000_000, transcendentals=0
        ),
    )(*ins)


def place(x, diagonal):
    return jnp.sum(jnp.where(diagonal, x, 0.0), axis=0, keepdims=True)


def pool_kernel(
    q_ref, k_ref, v_ref, q1_ref, kv1_ref, q2_ref, kv2_ref, send_ref, one_s, two_s, three_s
):
    low = low_lanes(32)
    low16 = low_lanes(16)
    level3 = []
    for index, ref in enumerate((q_ref, k_ref, v_ref)):
        one = halved(one_s.at[index], ref[...].astype(F32))
        two = halved(two_s.at[index], one.astype(F32))
        if index == 0:
            q1_ref[...] = one
            q2_ref[...] = two
        else:
            kv1_ref[index - 1] = one
            kv2_ref[index - 1] = two
        level3.append(halved(three_s.at[index], two.astype(F32)).astype(F32))
    q, k, v = level3
    qr, kr, vr = swap_halves(q), swap_halves(k), swap_halves(v)
    send_ref[0, 0:32, :] = jnp.where(low, k, vr).astype(BF16)
    send_ref[1, 0:32, :] = jnp.where(low, kr, v).astype(BF16)
    send_ref[0, 32:48, :] = jnp.where(low16, q[0:16], qr[16:32]).astype(BF16)
    send_ref[1, 32:48, :] = jnp.where(low16, qr[0:16], q[16:32]).astype(BF16)


def sibling_slots(me, level):
    bit = level - 5
    first = ((me >> bit) ^ 1) << bit
    return [first + i for i in range(1 << bit)]


def prepare_kernel(me_ref, recv_ref, q_ref, kv_ref, block_ref, send_ref):
    me = me_ref[0]
    low16 = low_lanes(16)
    for d in range(RING):
        kv_ref[32 * d : 32 * d + 32, :] = recv_ref[d, 0:32, :]
        packed = recv_ref[d, 32:48, :].astype(F32) * 0.125
        q_ref[32 * d : 32 * d + 16, :] = jnp.where(low16, packed, 0.0).astype(BF16)
        q_ref[32 * d + 16 : 32 * d + 32, :] = jnp.where(
            low16, swap_halves(packed), 0.0
        ).astype(BF16)
    for level in range(3, 8):
        rows = ROWS[level]
        step = min(rows, 256)
        matrix = pool_matrix(step // 2)
        for start in range(0, rows, step):
            source = slice(FIRST[level] + start, FIRST[level] + start + step)
            at = FIRST[level + 1] + start // 2
            target = slice(at, at + step // 2)
            q_ref[target, :] = dot(matrix, q_ref[source, :]).astype(BF16)
            kv_ref[target, :] = dot(matrix, kv_ref[source, :]).astype(BF16)
    end = FIRST[8] + ROWS[8]
    q_ref[end:STACK, :] = jnp.zeros((STACK - end, LANES), BF16)
    kv_ref[end:STACK, :] = jnp.zeros((STACK - end, LANES), BF16)
    block_ref[...] = kv_ref[FIRST[5] : FIRST[5] + B, :]
    send_ref[...] = jnp.zeros_like(send_ref)
    for level in range(6, 9):
        rows = ROWS[level]
        block = kv_ref[FIRST[level] : FIRST[level] + rows, :]
        for slot in sibling_slots(me, level):
            send_ref[slot, 0:rows, :] = block


def heads_forward(pairs, bias):
    heads = []
    for q, k, v in pairs:
        low_q = low_lanes(q.shape[0])
        low_v = low_lanes(v.shape[0])
        scaled = q.astype(F32) * 0.125
        values = v.astype(F32)
        for mine_q, mine_v in (
            (low_q, low_v),
            (jnp.logical_not(low_q), jnp.logical_not(low_v)),
        ):
            heads.append(
                (
                    jnp.where(mine_q, scaled, 0.0).astype(BF16),
                    k,
                    jnp.where(mine_v, values, 1.0).astype(BF16),
                )
            )
    scores = [dot_nt(q, k) for q, k, _ in heads]
    tops = [jnp.max(s, axis=1, keepdims=True) for s in scores]
    raised = [jnp.exp(s - top).astype(BF16) for s, top in zip(scores, tops)]
    sums = [dot(r, head[2]) for r, head in zip(raised, heads)]
    results = []
    for p, (q, _, _) in enumerate(pairs):
        low = low_lanes(q.shape[0])
        weighted = jnp.where(low, sums[2 * p], sums[2 * p + 1])
        total = swap_halves(jnp.where(low, sums[2 * p + 1], sums[2 * p]))
        top = jnp.where(low, tops[2 * p], tops[2 * p + 1])
        results.append((weighted / total, top + jnp.log(total) + bias))
    return results


def own_forward_kernel(steps):
    pairs = [(q[...], k[...], v[...]) for q, k, v, _, _ in steps]
    for views, (att, lse) in zip(steps, heads_forward(pairs, 0.0)):
        views[3][...] = att
        views[4][...] = lse


def core_forward_kernel(steps):
    pairs = [(q[...], kv[0], kv[1]) for q, kv, _, _ in steps]
    for views, (att, lse) in zip(steps, heads_forward(pairs, LN2)):
        views[2][...] = att
        views[3][...] = lse


def ring_pair(kva, kvb):
    return (
        jnp.concatenate([kva[0], kvb[0]], axis=0),
        jnp.concatenate([kva[1], kvb[1]], axis=0),
    )


def ring_forward_kernel(steps):
    pairs = [(q[...],) + ring_pair(kva, kvb) for q, kva, kvb, _, _ in steps]
    for views, (att, lse) in zip(steps, heads_forward(pairs, 2.0 * LN2)):
        views[3][...] = att
        views[4][...] = lse


def attend(q, kv, level):
    s = dot_nt(q, kv)
    top = jnp.max(s, axis=1, keepdims=True)
    raised = jnp.exp(s - top)
    ones = jnp.where(low_lanes(B), 1.0, kv.astype(F32)).astype(BF16)
    tops = jnp.broadcast_to(top + level * LN2, (q.shape[0], LANES))
    return tops, dot(raised.astype(BF16), ones)


def join(top_a, sum_a, top_b, sum_b):
    high = jnp.maximum(top_a, top_b)
    return high, jnp.exp(top_a - high) * sum_a + jnp.exp(top_b - high) * sum_b


def head_forward_kernel(q_ref, kv_ref, top_ref, sum_ref):
    tops, sums = None, None
    double = spread_matrix(64, 2)
    for level in (4, 3):
        new_tops, new_sums = [], []
        for block in range(ROWS[level] // B):
            at = FIRST[level] + B * block
            beside = FIRST[level] + B * (block ^ 1)
            top, total = attend(q_ref[at : at + B, :], kv_ref[beside : beside + B, :], level)
            if tops is not None:
                half = slice(64 * (block % 2), 64 * (block % 2) + 64)
                up_top = spread(double, tops[block // 2][half], 3)
                up_sum = spread(double, sums[block // 2][half], 2)
                top, total = join(top, total, up_top, up_sum)
            new_sums.append(total)
            new_tops.append(top)
        tops, sums = new_tops, new_sums
    for block in range(4):
        top_ref[B * block : B * block + B, :] = tops[block]
        sum_ref[B * block : B * block + B, :] = sums[block]


def head_merge_kernel(
    me_ref, beside_ref, recv_ref, q_ref, top_ref, sum_ref, send_ref, sibling_ref
):
    me = me_ref[0]
    sibling_ref[0] = beside_ref[...]
    levels = (8, 7, 6, 5)
    for level in levels[:3]:
        rows = ROWS[level]
        for index, slot in enumerate(sibling_slots(me, level)):
            sibling_ref[level - 5, rows * index : rows * index + rows, :] = recv_ref[
                slot, 0:rows, :
            ]
    keys = [sibling_ref[level - 5] for level in levels]
    scores = [
        dot_nt(q_ref[FIRST[level] : FIRST[level] + ROWS[level], :], kv)
        for level, kv in zip(levels, keys)
    ]
    highest = [jnp.max(s, axis=1, keepdims=True) for s in scores]
    raised = [jnp.exp(s - top).astype(BF16) for s, top in zip(scores, highest)]
    totals = [
        dot(r, jnp.where(low_lanes(B), 1.0, kv.astype(F32)).astype(BF16))
        for r, kv in zip(raised, keys)
    ]
    tops, sums = None, None
    for level, top, total in zip(levels, highest, totals):
        rows = ROWS[level]
        top = jnp.broadcast_to(top + level * LN2, (rows, LANES))
        if tops is not None:
            double = spread_matrix(rows // 2, 2)
            top, total = join(top, total, spread(double, tops, 3), spread(double, sums, 2))
        tops, sums = top, total
    low = low_lanes(B)
    low16 = low_lanes(16)
    diagonal = lax.broadcasted_iota(jnp.int32, (32, LANES), 0) == lane_of(32)
    four = spread_matrix(32, 4)
    tail = jnp.zeros((13, LANES), F32)
    spreads = [
        (spread(four, tops[32 * i : 32 * i + 32], 3), spread(four, sums[32 * i : 32 * i + 32], 2))
        for i in range(4)
    ]
    for i, (up_top, up_sum) in enumerate(spreads):
        at = slice(B * i, B * i + B)
        high, total = join(top_ref[at, :], sum_ref[at, :], up_top, up_sum)
        count = jnp.where(low, total, swap_halves(total))
        att = total / count
        lse = high + jnp.log(count)
        moved = swap_halves(att)
        for j in range(4):
            d = 4 * i + j
            r = 32 * j
            send_ref[d, 0:16, :] = jnp.where(
                low16, moved[r : r + 16], att[r + 16 : r + 32]
            ).astype(BF16)
            line = place(lse[r : r + 32], diagonal)
            parts = [part.astype(F32) for part in pieces(line, 3)]
            send_ref[d, 16:32, :] = jnp.concatenate(parts + [tail], axis=0).astype(BF16)


def combine_kernel(
    att0_ref, lse0_ref, att1_ref, lse1_ref, att2_ref, lse2_ref, recv_ref, grad_ref,
    out_ref, stat_ref, stat1_ref, g1_ref, stat2_ref, g2_ref, send_ref,
    lse_s, grad_s, align_s, r_s, g_s, f_s, r2_s, g2_s, f2_s, up_s,
):
    low16 = low_lanes(16)
    r = lax.broadcasted_iota(jnp.int32, (LANES, LANES), 0)
    c = lax.broadcasted_iota(jnp.int32, (LANES, LANES), 1)
    per_head = jnp.where(r >> 6 == c >> 6, 1.0, 0.0).astype(BF16)
    own = lax.broadcasted_iota(jnp.int32, (32, LANES), 0) == lane_of(32)

    packed_a = recv_ref[0].astype(F32)
    packed_b = recv_ref[1].astype(F32)
    rows_a, rows_b = packed_a[0:16], packed_b[0:16]
    att3 = jnp.concatenate(
        [
            jnp.where(low16, rows_a, swap_halves(rows_b)),
            jnp.where(low16, swap_halves(rows_a), rows_b),
        ],
        axis=0,
    )
    columns = []
    for packed in (packed_a, packed_b):
        line = packed[16:17] + packed[17:18] + packed[18:19]
        columns.append(jnp.sum(jnp.where(own, line, 0.0), axis=1, keepdims=True))
    lse = jnp.where(low_lanes(32), columns[0], columns[1])
    att = att3
    for index, (att_ref, lse_ref) in enumerate(
        ((att2_ref, lse2_ref), (att1_ref, lse1_ref), (att0_ref, lse0_ref))
    ):
        att = repeated(up_s.at[2 * index], att, 2)
        lse = repeated(up_s.at[2 * index + 1], lse, 2)
        own_lse = lse_ref[...]
        high = jnp.maximum(lse, own_lse)
        e_up = jnp.exp(lse - high)
        e_own = jnp.exp(own_lse - high)
        den = e_up + e_own
        att = (e_up * att + e_own * att_ref[...]) / den
        lse = high + jnp.log(den)
    attended = att.astype(BF16)
    full = lse
    out_ref[...] = attended
    grad = grad_ref[...].astype(F32)
    product = grad * attended.astype(F32)
    align = None
    for part in pieces(product, 3):
        term = dot(part, per_head)
        align = term if align is None else align + term
    stat_ref[...] = jnp.where(lane_of(256) & 32 == 0, full, align)
    lse_s[...] = full
    grad_s[...] = grad
    align_s[...] = align

    def fold(lse, grads, aligns, rows):
        a, b = pl.ds(0, rows, stride=2), pl.ds(1, rows, stride=2)
        la, lb = lse[a, :], lse[b, :]
        least = jnp.minimum(la, lb)
        ea, eb = jnp.exp(least - la), jnp.exp(least - lb)
        return (
            least,
            ea * grads[a, :] + eb * grads[b, :],
            ea * aligns[a, :] + eb * aligns[b, :],
        )

    r1, g1, f1 = fold(lse_s, grad_s, align_s, 128)
    stat1_ref[...] = jnp.where(lane_of(B) & 32 == 0, r1, f1)
    g1_ref[...] = g1.astype(BF16)
    r_s[...] = r1
    g_s[...] = g1
    f_s[...] = f1
    r2, g2, f2 = fold(r_s, g_s, f_s, 64)
    stat2_ref[...] = jnp.where(lane_of(64) & 32 == 0, r2, f2)
    g2_ref[...] = g2.astype(BF16)
    r2_s[...] = r2
    g2_s[...] = g2
    f2_s[...] = f2
    r3, g3, f3 = fold(r2_s, g2_s, f2_s, 32)
    row32 = lax.broadcasted_iota(jnp.int32, (32, LANES), 0)
    diagonal = row32 == (lane_of(32) & (E - 1))
    line_r = place(r3, diagonal)
    line_f = place(f3, diagonal)
    low1 = low_lanes(1)
    wide_r = jnp.broadcast_to(line_r, (8, LANES))
    wide_f = jnp.broadcast_to(line_f, (8, LANES))
    lines = (
        jnp.where(low1, line_r, swap_halves(wide_f)[0:1]),
        jnp.where(low1, swap_halves(wide_r)[0:1], line_f),
    )
    moved = swap_halves(g3)
    tail = jnp.zeros((13, LANES), F32)
    send_ref[0, 0:16, :] = jnp.where(low16, g3[0:16], moved[16:32]).astype(BF16)
    send_ref[1, 0:16, :] = jnp.where(low16, moved[0:16], g3[16:32]).astype(BF16)
    for j in range(2):
        parts = [part.astype(F32) for part in pieces(lines[j], 3)]
        send_ref[j, 16:32, :] = jnp.concatenate(parts + [tail], axis=0).astype(BF16)


def level_backward(q, kv, least, grads, level):
    rows = q.shape[0]
    low = low_lanes(rows)
    s = dot_nt(q, kv)
    weight = jnp.exp(s + (level * LN2 - least[:, 0:1]))
    cograd = jnp.where(low, 0.0, grads).astype(BF16)
    slope = (weight * (dot_nt(cograd, kv) - grads[:, 0:1])).astype(BF16)
    query_part = dot(slope, kv) * 0.125
    other_part = dot_tn(slope, q) + dot_tn(weight.astype(BF16), cograd)
    return query_part, other_part


def unpack_and_fold(recv_ref, r_ref, g_ref, last):
    low = low_lanes(32)
    row32 = lax.broadcasted_iota(jnp.int32, (32, LANES), 0)
    first = row32 == lane_of(32)
    second = row32 + E == lane_of(32)
    for d in range(RING):
        packed = recv_ref[d].astype(F32)
        line = packed[16:17] + packed[17:18] + packed[18:19]
        least = jnp.sum(jnp.where(first, line, 0.0), axis=1, keepdims=True)
        flow = jnp.sum(jnp.where(second, line, 0.0), axis=1, keepdims=True)
        grads = jnp.concatenate([swap_halves(packed[0:16]), packed[0:16]], axis=0)
        r_ref[32 * d : 32 * d + 32, :] = jnp.broadcast_to(least, (32, LANES))
        g_ref[32 * d : 32 * d + 32, :] = jnp.where(low, flow, grads)
    for level in range(3, last):
        rows = ROWS[level + 1]
        a = pl.ds(FIRST[level], rows, stride=2)
        b = pl.ds(FIRST[level] + 1, rows, stride=2)
        la, lb = r_ref[a, :], r_ref[b, :]
        least = jnp.minimum(la, lb)
        to = slice(FIRST[level + 1], FIRST[level + 1] + rows)
        r_ref[to, :] = least
        g_ref[to, :] = jnp.exp(least - la) * g_ref[a, :] + jnp.exp(least - lb) * g_ref[b, :]


def head_top_kernel(
    me_ref, recv_ref, q_ref, sibling_ref, q5_ref, beside_ref, send_ref, r_ref, g_ref
):
    me = me_ref[0]
    unpack_and_fold(recv_ref, r_ref, g_ref, 8)
    send_ref[...] = jnp.zeros_like(send_ref)
    running = None
    for level in (8, 7, 6, 5):
        rows = ROWS[level]
        at = slice(FIRST[level], FIRST[level] + rows)
        query_part, other_part = level_backward(
            q_ref[at, :], sibling_ref[level - 5], r_ref[at, :], g_ref[at, :], level
        )
        other_part = other_part.astype(BF16)
        if level == 5:
            beside_ref[...] = other_part
        for index, slot in enumerate(sibling_slots(me, level) if level > 5 else ()):
            send_ref[slot, 0:rows, :] = other_part[rows * index : rows * index + rows]
        if running is None:
            running = query_part
        else:
            running = query_part + spread(spread_matrix(rows // 2, 2, 0.5), running, 2)
    q5_ref[...] = running


def head_low_kernel(q_ref, kv_ref, recv_ref, q5_ref, query_ref, other_ref, r_ref, g_ref):
    unpack_and_fold(recv_ref, r_ref, g_ref, 4)
    double = spread_matrix(64, 2, 0.5)
    query_up = [q5_ref[...]]
    other_up = None
    for level in (4, 3):
        blocks = ROWS[level] // B
        query_parts = [None] * blocks
        other_parts = [None] * blocks
        for block in range(blocks):
            at = FIRST[level] + B * block
            beside = FIRST[level] + B * (block ^ 1)
            query_part, other_part = level_backward(
                q_ref[at : at + B, :],
                kv_ref[beside : beside + B, :],
                r_ref[at : at + B, :],
                g_ref[at : at + B, :],
                level,
            )
            query_parts[block] = query_part
            other_parts[block ^ 1] = other_part
        for block in range(blocks):
            half = slice(64 * (block % 2), 64 * (block % 2) + 64)
            query_parts[block] = query_parts[block] + spread(
                double, query_up[block // 2][half], 2
            )
            if other_up is not None:
                other_parts[block] = other_parts[block] + spread(
                    double, other_up[block // 2][half], 2
                )
        query_up, other_up = query_parts, other_parts
    for block in range(4):
        query_ref[B * block : B * block + B, :] = query_up[block]
        other_ref[B * block : B * block + B, :] = other_up[block]


def head_last_kernel(me_ref, beside_ref, recv_ref, query_ref, other_ref, send_ref):
    me = me_ref[0]
    running = None
    for level in (8, 7, 6):
        rows = ROWS[level]
        total = None
        for slot in sibling_slots(me, level):
            term = recv_ref[slot, 0:rows, :].astype(F32)
            total = term if total is None else total + term
        if running is not None:
            total = total + spread(spread_matrix(rows // 2, 2, 0.5), running, 2)
        running = total
    running = beside_ref[...].astype(F32) + spread(spread_matrix(64, 2, 0.5), running, 2)
    four = spread_matrix(8, 4, 0.25)
    low16 = low_lanes(16)
    for d in range(RING):
        at = slice(32 * d, 32 * d + 32)
        other = other_ref[at, :] + spread(four, running[8 * d : 8 * d + 8], 2)
        query = query_ref[at, :]
        send_ref[d, 0:32, :] = other.astype(BF16)
        send_ref[d, 32:48, :] = jnp.where(
            low16, query[0:16], swap_halves(query)[16:32]
        ).astype(BF16)


def heads_backward(pairs, bias):
    heads = []
    scaled_pairs = []
    for q, k, v, grads, stat in pairs:
        low_q = low_lanes(q.shape[0])
        scaled = q.astype(F32) * 0.125
        wide = grads.astype(F32)
        scaled_pairs.append(scaled.astype(BF16))
        for j in range(2):
            mine = low_q if j == 0 else jnp.logical_not(low_q)
            heads.append(
                (
                    jnp.where(mine, scaled, 0.0).astype(BF16),
                    k,
                    jnp.where(mine, wide, 0.0).astype(BF16),
                    v,
                    bias - stat[:, E * j : E * j + 1],
                    stat[:, E * j + 32 : E * j + 33],
                )
            )
    scores = [dot_nt(head[0], head[1]) for head in heads]
    through = [dot_nt(head[2], head[3]) for head in heads]
    weights = [jnp.exp(s + head[4]) for s, head in zip(scores, heads)]
    slopes = [
        (w * (t - head[5])).astype(BF16) for w, t, head in zip(weights, through, heads)
    ]
    weights = [w.astype(BF16) for w in weights]
    results = []
    for p, (q, k, _, grads, _) in enumerate(pairs):
        low_q = low_lanes(q.shape[0])
        low_k = low_lanes(k.shape[0])
        one, two = slopes[2 * p : 2 * p + 2]
        results.append(
            (
                jnp.where(low_q, dot(one, k), dot(two, k)) * 0.125,
                jnp.where(
                    low_k, dot_tn(one, scaled_pairs[p]), dot_tn(two, scaled_pairs[p])
                ),
                jnp.where(
                    low_k, dot_tn(weights[2 * p], grads), dot_tn(weights[2 * p + 1], grads)
                ),
            )
        )
    return results


def own_backward_kernel(steps):
    pairs = [tuple(view[...] for view in views[:5]) for views in steps]
    for views, grads in zip(steps, heads_backward(pairs, 0.0)):
        for view, value in zip(views[5:], grads):
            view[...] = value


def core_backward_kernel(steps):
    pairs = [(q[...], kv[0], kv[1], g[...], stat[...]) for q, kv, stat, g, _, _ in steps]
    for views, (dq, dk, dv) in zip(steps, heads_backward(pairs, LN2)):
        views[4][...] = dq
        views[5][0] = dk.astype(BF16)
        views[5][1] = dv.astype(BF16)


def ring_backward_kernel(steps):
    pairs = [
        (views[0][...],) + ring_pair(views[1], views[2]) + (views[4][...], views[3][...])
        for views in steps
    ]
    for views, (dq, dk, dv) in zip(steps, heads_backward(pairs, 2.0 * LN2)):
        views[5][...] = dq
        views[6][0] = dk[0:64]
        views[6][1] = dv[0:64]
        views[7][0] = dk[64:128].astype(BF16)
        views[7][1] = dv[64:128].astype(BF16)


def final_kernel(
    dq_ref, dk_ref, dv_ref, dq1_ref, kv1_ref, dq2_ref, kv2_ref, recv_ref,
    q_out, k_out, v_out, quarter_s, half_s, full_s,
):
    low = low_lanes(32)
    low16 = low_lanes(16)
    a = recv_ref[0].astype(F32)
    b = recv_ref[1].astype(F32)
    ar, br = swap_halves(a), swap_halves(b)
    g3k = jnp.where(low, a[0:32], br[0:32])
    g3v = jnp.where(low, ar[0:32], b[0:32])
    g3q = jnp.concatenate(
        [
            jnp.where(low16, a[32:48], br[32:48]),
            jnp.where(low16, ar[32:48], b[32:48]),
        ],
        axis=0,
    )
    work = (
        (dq_ref, dq1_ref[...], dq2_ref[...], g3q, q_out),
        (dk_ref, kv1_ref[0].astype(F32), kv2_ref[0].astype(F32), g3k, k_out),
        (dv_ref, kv1_ref[1].astype(F32), kv2_ref[1].astype(F32), g3v, v_out),
    )
    for index, (own, one, two, three, out) in enumerate(work):
        two = two + repeated(quarter_s.at[index], three * 0.5, 2)
        one = one + repeated(half_s.at[index], two * 0.5, 2)
        out[...] = (own[...] + repeated(full_s.at[index], one * 0.5, 2)).astype(BF16)


def pairs_of(mask, size):
    return [(source, source ^ mask) for source in range(size)]


class Tall:
    def __init__(self, rows):
        self.rows = rows

    def spec(self, step):
        return pl.BlockSpec((self.rows, LANES * step), lambda p: (0, p))

    def view(self, ref, i):
        return ref.at[:, LANES * i : LANES * (i + 1)]


class TwoTall(Tall):
    def spec(self, step):
        return pl.BlockSpec((2, self.rows, LANES * step), lambda p: (0, 0, p))

    def view(self, ref, i):
        return ref.at[:, :, LANES * i : LANES * (i + 1)]


class Slots(Tall):
    def spec(self, step):
        return pl.BlockSpec((2 * step, self.rows, LANES), lambda p: (p, 0, 0))

    def view(self, ref, i):
        return ref.at[2 * i : 2 * i + 2]


def over_pairs(
    kernel, outs, out_kinds, ins, in_kinds, scratch=(), step=2, flops=1e9, moved=5e6,
    joint=False,
):
    kinds = in_kinds + out_kinds

    def body(*refs):
        if joint:
            kernel([[kind.view(ref, i) for kind, ref in zip(kinds, refs)] for i in range(step)])
            return
        for i in range(step):
            views = [kind.view(ref, i) for kind, ref in zip(kinds, refs)]
            kernel(*views, *[ref.at[i] for ref in refs[len(kinds) :]])

    return pl.pallas_call(
        body,
        grid=(PAIRS // step,),
        out_shape=[jax.ShapeDtypeStruct(s, d) for s, d in outs],
        in_specs=[kind.spec(step) for kind in in_kinds],
        out_specs=[kind.spec(step) for kind in out_kinds],
        scratch_shapes=[pltpu.VMEM((step,) + shape + (LANES,), F32) for shape in scratch],
        compiler_params=pltpu.CompilerParams(vmem_limit_bytes=58 * 1024 * 1024),
        cost_estimate=pl.CostEstimate(
            flops=int(flops), bytes_accessed=int(moved), transcendentals=0
        ),
    )(*ins)


STEPS = {
    "pool": 4,
    "local_forward": 2,
    "combine": 4,
    "local_backward": 2,
    "final": 4,
    "core_forward": 4,
    "core_backward": 4,
}


def per_device(q, k, v, grad):
    size = lax.axis_size("seq")
    planes = size // RING
    rings = [[RING * g + i for i in range(RING)] for g in range(planes)]
    columns = [[RING * g + i for g in range(planes)] for i in range(RING)]
    me = (lax.axis_index("seq") // RING).astype(jnp.int32).reshape(1)
    rows, width = q.shape

    def exchange(x, groups):
        return lax.all_to_all(x, "seq", 0, 0, axis_index_groups=groups, tiled=True)

    def swapped(x, mask):
        return lax.ppermute(x, "seq", pairs_of(mask, size))

    quarter = (rows // 4, width)
    q1, kv1, q2, kv2, send1 = over_pairs(
        pool_kernel,
        [
            ((B, width), BF16),
            ((2, B, width), BF16),
            (quarter, BF16),
            ((2,) + quarter, BF16),
            ((RING, 48, LANES), BF16),
        ],
        [Tall(B), TwoTall(B), Tall(64), TwoTall(64), Slots(48)],
        (q, k, v),
        [Tall(rows)] * 3,
        scratch=((3, 256), (3, B), (3, 64)),
        step=STEPS["pool"],
    )
    kv1s = swapped(kv1, 1)
    recv1 = exchange(send1, rings)
    full = ((rows, width), F32)
    att0, lse0 = over_pairs(
        own_forward_kernel,
        [full, full],
        [Tall(rows)] * 2,
        (q, k, v),
        [Tall(rows)] * 3,
        step=STEPS["local_forward"],
        joint=True,
        flops=6e9,
        moved=1e7,
    )
    recv1, att0 = lax.optimization_barrier((recv1, att0))
    qh, kvh, block, sendx = call(
        prepare_kernel,
        [((STACK, LANES), BF16)] * 2 + [((B, LANES), BF16), ((RING, 64, LANES), BF16)],
        (me, recv1),
        smem_first=True,
    )
    sendx, kv2 = lax.optimization_barrier((sendx, kv2))
    beside = swapped(block, RING)
    kv2a = swapped(kv2, 2)
    kv2b = swapped(kv2a, 1)
    recvx = exchange(sendx, columns)
    half = (B, width)
    att1, lse1 = over_pairs(
        core_forward_kernel,
        [(half, F32)] * 2,
        [Tall(B)] * 2,
        (q1, kv1s),
        [Tall(B), TwoTall(B)],
        step=STEPS["core_forward"],
        joint=True,
        flops=2e9,
    )
    tops, sums = call(
        head_forward_kernel, [((512, LANES), F32)] * 2, (qh, kvh), flops=1e9
    )
    recvx, att1 = lax.optimization_barrier((recvx, att1))
    send2, siblings = call(
        head_merge_kernel,
        [((RING, 32, LANES), BF16), ((4, B, LANES), BF16)],
        (me, beside, recvx, qh, tops, sums),
        smem_first=True,
    )
    send2, q2_later = lax.optimization_barrier((send2, q2))
    recv2 = exchange(send2, rings)
    att2, lse2 = over_pairs(
        ring_forward_kernel,
        [(quarter, F32)] * 2,
        [Tall(64)] * 2,
        (q2_later, kv2a, kv2b),
        [Tall(64), TwoTall(64), TwoTall(64)],
        step=STEPS["core_forward"],
        joint=True,
        flops=2e9,
    )
    attended, stat, stat1, g1, stat2, g2, send3 = over_pairs(
        combine_kernel,
        [
            ((rows, width), BF16),
            full,
            (half, F32),
            (half, BF16),
            (quarter, F32),
            (quarter, BF16),
            ((RING, 32, LANES), BF16),
        ],
        [Tall(rows)] * 2 + [Tall(B)] * 2 + [Tall(64)] * 2 + [Slots(32)],
        (att0, lse0, att1, lse1, att2, lse2, recv2, grad),
        [Tall(rows)] * 2 + [Tall(B)] * 2 + [Tall(64)] * 2 + [Slots(32), Tall(rows)],
        scratch=((256,),) * 3 + ((B,),) * 3 + ((64,),) * 3 + ((6, 256),),
        step=STEPS["combine"],
    )
    recv3 = exchange(send3, rings)
    dq2, same, across = over_pairs(
        ring_backward_kernel,
        [(quarter, F32), ((2,) + quarter, F32), ((2,) + quarter, BF16)],
        [Tall(64), TwoTall(64), TwoTall(64)],
        (q2, kv2a, kv2b, stat2, g2),
        [Tall(64), TwoTall(64), TwoTall(64), Tall(64), Tall(64)],
        step=STEPS["core_backward"],
        joint=True,
        flops=3e9,
    )
    recv3, dq2 = lax.optimization_barrier((recv3, dq2))
    partner = swapped(across, 1)
    back2 = swapped((same + partner.astype(F32)).astype(BF16), 2)
    stack = [pltpu.VMEM((STACK, LANES), F32)] * 2
    q5, part5, sendy = call(
        head_top_kernel,
        [((B, LANES), F32), ((B, LANES), BF16), ((RING, 64, LANES), BF16)],
        (me, recv3, qh, siblings),
        scratch=stack,
        smem_first=True,
    )
    part5, q1_late = lax.optimization_barrier((part5, q1))
    beside_grad = swapped(part5, RING)
    recvy = exchange(sendy, columns)
    query_low, other_low = call(
        head_low_kernel,
        [((512, LANES), F32)] * 2,
        (qh, kvh, recv3, q5),
        scratch=stack,
        flops=2e9,
    )
    dq1, dkv1 = over_pairs(
        core_backward_kernel,
        [(half, F32), ((2, B, width), BF16)],
        [Tall(B), TwoTall(B)],
        (q1_late, kv1s, stat1, g1),
        [Tall(B), TwoTall(B)] + [Tall(B)] * 2,
        step=STEPS["core_backward"],
        joint=True,
        flops=3e9,
    )
    back1 = swapped(dkv1, 1)
    recvy, dq1 = lax.optimization_barrier((recvy, dq1))
    (send4,) = call(
        head_last_kernel,
        [((RING, 48, LANES), BF16)],
        (me, beside_grad, recvy, query_low, other_low),
        smem_first=True,
    )
    recv4 = exchange(send4, rings)
    dq, dk, dv = over_pairs(
        own_backward_kernel,
        [full] * 3,
        [Tall(rows)] * 3,
        (q, k, v, grad, stat),
        [Tall(rows)] * 5,
        step=STEPS["local_backward"],
        joint=True,
        flops=9e9,
        moved=1e7,
    )
    query_grad, key_grad, value_grad = over_pairs(
        final_kernel,
        [((rows, width), BF16)] * 3,
        [Tall(rows)] * 3,
        (dq, dk, dv, dq1, back1, dq2, back2, recv4),
        [Tall(rows)] * 3 + [Tall(B), TwoTall(B), Tall(64), TwoTall(64), Slots(48)],
        scratch=((3, 64), (3, B), (3, 256)),
        step=STEPS["final"],
    )
    return attended, query_grad, key_grad, value_grad


def solution(mesh):
    return jax.shard_map(
        per_device,
        mesh=mesh,
        in_specs=(P("seq", None),) * 4,
        out_specs=(P("seq", None),) * 4,
        check_vma=False,
    )
```

profile of v0, /device:TPU:1, one launch (start us, length us, event | category | flops | bytes accessed | tf_op | source)
XLA Modules:
  0.0 110.5 jit_solution(9921232538923175851)
XLA Ops:
  0.6 2.9 %shard_map.75 = (bf16[128,1024]{1,0:T(8,128)(2,1)}, bf16[2,128,1024]{2,1,0:T(8,128)(2,1)}, bf16[64,1024]{1,0:T(8,128)(2,1)}, bf16[2,64,1024]{2,1,0:T(8,128)(2,1)}, bf16[16,48,128]{2,1,0:T(8,128)(2,1)}) custom-call(bf16[256,1024]{1,0:T(8,128)(2,1)} %refs_0_.5, bf16[256,1024]{1,0:T(8,128)(2,1)} %refs_1_.5, bf16[256,1024]{1,0:T(8,128)(2,1)} %refs_2_.5), custom_call_target="tpu_custom_call" | custom-call | flops 1000000000 | bytes 5000000 | tf_op jit(solution)/shard_map/pallas_call | solution.py:702
  3.5 10.0 %all-to-all-start = ((bf16[16,48,128]{2,1,0:T(8,128)(2,1)}), bf16[16,48,128]{2,1,0:T(8,128)(2,1)S(1)}, u32[]{:S(2)}, u32[]{:S(2)}) async-start(bf16[16,48,128]{2,1,0:T(8,128)(2,1)} %get-tuple-element.60), calls=%async_computation | async-start | bytes 393216 | tf_op jit(solution)/shard_map/all_to_all | solution.py:736
  13.7 5.0 %shard_map.76 = (f32[256,1024]{1,0:T(8,128)}, f32[256,1024]{1,0:T(8,128)}) custom-call(bf16[256,1024]{1,0:T(8,128)(2,1)} %refs_0_.5, bf16[256,1024]{1,0:T(8,128)(2,1)} %refs_1_.5, bf16[256,1024]{1,0:T(8,128)(2,1)} %refs_2_.5), custom_call_target="tpu_custom_call" | custom-call | flops 6000000000 | bytes 10000000 | tf_op jit(solution)/shard_map/pallas_call | solution.py:702
  18.7 5.1 %all-to-all-done.recv_ref = bf16[16,48,128]{2,1,0:T(8,128)(2,1)S(1)} async-done(((bf16[16,48,128]{2,1,0:T(8,128)(2,1)}), bf16[16,48,128]{2,1,0:T(8,128)(2,1)S(1)}, u32[]{:S(2)}, u32[]{:S(2)}) %all-to-all-start) | async-done | bytes 196640 | tf_op jit(solution)/shard_map/all_to_all | solution.py:736
  23.8 1.5 %shard_map.77 = (bf16[1024,128]{1,0:T(8,128)(2,1)S(1)}, bf16[1024,128]{1,0:T(8,128)(2,1)S(1)}, bf16[128,128]{1,0:T(8,128)(2,1)S(1)}, bf16[16,64,128]{2,1,0:T(8,128)(2,1)}) custom-call(s32[1]{0:T(128)} %bitcast.me_ref, bf16[16,48,128]{2,1,0:T(8,128)(2,1)S(1)} %all-to-all-done.recv_ref), custom_call_target="tpu_custom_call" | custom-call | flops 100000000 | bytes 2000000 | tf_op jit(solution)/shard_map/pallas_call | solution.py:102
  25.3 6.8 %all-to-all-start.1 = ((bf16[16,64,128]{2,1,0:T(8,128)(2,1)}), bf16[16,64,128]{2,1,0:T(8,128)(2,1)S(1)}, u32[]{:S(2)}, u32[]{:S(2)}) async-start(bf16[16,64,128]{2,1,0:T(8,128)(2,1)} %get-tuple-element.67), calls=%async_computation.1 | async-start | bytes 524288 | tf_op jit(solution)/shard_map/all_to_all | solution.py:736
  32.1 1.4 %collective-permute-start.1 = (bf16[128,128]{1,0:T(8,128)(2,1)S(1)}, bf16[128,128]{1,0:T(8,128)(2,1)S(1)}, u32[]{:S(2)}, u32[]{:S(2)}) collective-permute-start(bf16[128,128]{1,0:T(8,128)(2,1)S(1)} %get-tuple-element.73), channel_id=1, source_target_pairs={{0,16},{1,17},{2,18},{3,19},{4,20},{5,21},{6,22},{7,23},{8,24},{9,... | collective-permute-start | bytes 98312 | tf_op jit(solution)/shard_map/ppermute | solution.py:739
  33.5 1.1 collective-permute-start.3
  34.5 1.1 %shard_map.79 = (f32[512,128]{1,0:T(8,128)S(1)}, f32[512,128]{1,0:T(8,128)S(1)}) custom-call(bf16[1024,128]{1,0:T(8,128)(2,1)S(1)} %get-tuple-element.75.q_ref, bf16[1024,128]{1,0:T(8,128)(2,1)S(1)} %get-tuple-element.76.kv_ref), custom_call_target="tpu_custom_call" | custom-call | flops 1000000000 | bytes 2000000 | tf_op jit(solution)/shard_map/pallas_call | solution.py:102
  35.7 0.8 copy-done.5
  36.5 3.1 %shard_map.78 = (f32[128,1024]{1,0:T(8,128)}, f32[128,1024]{1,0:T(8,128)}) custom-call(bf16[128,1024]{1,0:T(8,128)(2,1)} %get-tuple-element.99.refs_0_, bf16[2,128,1024]{2,1,0:T(8,128)(2,1)} %copy-done.5), custom_call_target="tpu_custom_call" | custom-call | flops 2000000000 | bytes 5000000 | tf_op jit(solution)/shard_map/pallas_call | solution.py:702
  39.6 0.8 all-to-all-done.1.recv_ref
  40.4 1.9 %shard_map.80 = (bf16[16,32,128]{2,1,0:T(8,128)(2,1)}, bf16[4,128,128]{2,1,0:T(8,128)(2,1)S(1)}) custom-call(s32[1]{0:T(128)} %bitcast.me_ref, bf16[128,128]{1,0:T(8,128)(2,1)S(1)} %collective-permute-done.1.beside_ref, bf16[16,64,128]{2,1,0:T(8,128)(2,1)S(1)} %all-to-all-done.1.recv_ref, bf16[1024,128]{1,0:T(8,128)(2,1)S(1)} %get-tuple-element.75.q_ref, ...), custom_call_target="tpu_custom_call" | custom-call | flops 100000000 | bytes 2000000 | tf_op jit(solution)/shard_map/pallas_call | solution.py:102
  42.3 5.0 %all-to-all-start.2 = ((bf16[16,32,128]{2,1,0:T(8,128)(2,1)}), bf16[16,32,128]{2,1,0:T(8,128)(2,1)S(1)}, u32[]{:S(2)}, u32[]{:S(2)}) async-start(bf16[16,32,128]{2,1,0:T(8,128)(2,1)} %get-tuple-element.85), calls=%async_computation.2 | async-start | bytes 262144 | tf_op jit(solution)/shard_map/all_to_all | solution.py:736
  47.3 0.7 copy-done.8
  48.0 2.9 %shard_map.81 = (f32[64,1024]{1,0:T(8,128)}, f32[64,1024]{1,0:T(8,128)}) custom-call(bf16[64,1024]{1,0:T(8,128)(2,1)} %get-tuple-element.81.refs_0_, bf16[2,64,1024]{2,1,0:T(8,128)(2,1)} %copy-done.6, bf16[2,64,1024]{2,1,0:T(8,128)(2,1)} %copy-done.8), custom_call_target="tpu_custom_call" | custom-call | flops 2000000000 | bytes 5000000 | tf_op jit(solution)/shard_map/pallas_call | solution.py:702
  51.0 5.5 %all-to-all-done.2.refs_6_ = bf16[16,32,128]{2,1,0:T(8,128)(2,1)S(1)} async-done(((bf16[16,32,128]{2,1,0:T(8,128)(2,1)}), bf16[16,32,128]{2,1,0:T(8,128)(2,1)S(1)}, u32[]{:S(2)}, u32[]{:S(2)}) %all-to-all-start.2) | async-done | bytes 131104 | tf_op jit(solution)/shard_map/all_to_all | solution.py:736
  57.2 5.8 %shard_map.82 = (bf16[256,1024]{1,0:T(8,128)(2,1)}, f32[256,1024]{1,0:T(8,128)}, f32[128,1024]{1,0:T(8,128)}, bf16[128,1024]{1,0:T(8,128)(2,1)}, f32[64,1024]{1,...) custom-call(f32[256,1024]{1,0:T(8,128)} %get-tuple-element.62.refs_0_, ...), custom_call_target="tpu_custom_call" | custom-call | flops 1000000000 | bytes 5000000 | tf_op jit(solution)/shard_map/pallas_call | solution.py:702
  63.0 3.4 %all-to-all-start.3 = ((bf16[16,32,128]{2,1,0:T(8,128)(2,1)}), bf16[16,32,128]{2,1,0:T(8,128)(2,1)S(1)}, u32[]{:S(2)}, u32[]{:S(2)}) async-start(bf16[16,32,128]{2,1,0:T(8,128)(2,1)} %get-tuple-element.91), calls=%async_computation.3 | async-start | bytes 262144 | tf_op jit(solution)/shard_map/all_to_all | solution.py:736
  66.4 3.5 %shard_map.84 = (f32[64,1024]{1,0:T(8,128)}, f32[2,64,1024]{2,1,0:T(8,128)}, bf16[2,64,1024]{2,1,0:T(8,128)(2,1)}) custom-call(bf16[64,1024]{1,0:T(8,128)(2,1)} %get-tuple-element.81.refs_0_, bf16[2,64,1024]{2,1,0:T(8,128)(2,1)} %copy-done.6, bf16[2,64,1024]{2,1,0:T(8,128)(2,1)} %copy-done.8, f32[64,1024]{1,0:T(8,128)} %get-tuple-element.92.refs_3_, ...), custom_call_target="tpu_custom_call" | custom-call | flops 3000000000 | bytes 5000000 | tf_op jit(solution)/shard_map/pallas_call | solution.py:702
  69.9 5.0 %all-to-all-done.3.recv_ref = bf16[16,32,128]{2,1,0:T(8,128)(2,1)S(1)} async-done(((bf16[16,32,128]{2,1,0:T(8,128)(2,1)}), bf16[16,32,128]{2,1,0:T(8,128)(2,1)S(1)}, u32[]{:S(2)}, u32[]{:S(2)}) %all-to-all-start.3) | async-done | bytes 131104 | tf_op jit(solution)/shard_map/all_to_all | solution.py:736
  74.9 1.9 %shard_map.85 = (f32[128,128]{1,0:T(8,128)S(1)}, bf16[128,128]{1,0:T(8,128)(2,1)S(1)}, bf16[16,64,128]{2,1,0:T(8,128)(2,1)}) custom-call(s32[1]{0:T(128)} %bitcast.me_ref, bf16[16,32,128]{2,1,0:T(8,128)(2,1)S(1)} %all-to-all-done.3.recv_ref, bf16[1024,128]{1,0:T(8,128)(2,1)S(1)} %get-tuple-element.75.q_ref, ...), custom_call_target="tpu_custom_call" | custom-call | flops 100000000 | bytes 2000000 | tf_op jit(solution)/shard_map/pallas_call | solution.py:102
  76.8 4.5 %all-to-all-start.4 = ((bf16[16,64,128]{2,1,0:T(8,128)(2,1)}), bf16[16,64,128]{2,1,0:T(8,128)(2,1)S(1)}, u32[]{:S(2)}, u32[]{:S(2)}) async-start(bf16[16,64,128]{2,1,0:T(8,128)(2,1)} %get-tuple-element.97), calls=%async_computation.4 | async-start | bytes 524288 | tf_op jit(solution)/shard_map/all_to_all | solution.py:736
  81.3 1.4 %collective-permute-start.7 = (bf16[128,128]{1,0:T(8,128)(2,1)S(1)}, bf16[128,128]{1,0:T(8,128)(2,1)S(1)}, u32[]{:S(2)}, u32[]{:S(2)}) collective-permute-start(bf16[128,128]{1,0:T(8,128)(2,1)S(1)} %get-tuple-element.108), channel_id=1, source_target_pairs={{0,16},{1,17},{2,18},{3,19},{4,20},{5,21},{6,22},{7,23},{8,24},{9,... | collective-permute-start | bytes 98312 | tf_op jit(solution)/shard_map/ppermute | solution.py:739
  82.6 3.6 %shard_map.86 = (f32[128,1024]{1,0:T(8,128)}, bf16[2,128,1024]{2,1,0:T(8,128)(2,1)}) custom-call(bf16[128,1024]{1,0:T(8,128)(2,1)} %get-tuple-element.99.refs_0_, bf16[2,128,1024]{2,1,0:T(8,128)(2,1)} %copy-done.5, f32[128,1024]{1,0:T(8,128)} %get-tuple-element.100.refs_2_, bf16[128,1024]{1,0:T(8,128)(2,1)} %get-tuple-element.101.refs_3_), custom_call_target="tpu_custom_call" | custom-call | flops 3000000000 | bytes 5000000 | tf_op jit(solution)/shard_map/pallas_call | solution.py:702
  86.2 0.8 collective-permute-start.4
  87.0 1.9 %shard_map.87 = (f32[512,128]{1,0:T(8,128)S(1)}, f32[512,128]{1,0:T(8,128)S(1)}) custom-call(bf16[1024,128]{1,0:T(8,128)(2,1)S(1)} %get-tuple-element.75.q_ref, bf16[1024,128]{1,0:T(8,128)(2,1)S(1)} %get-tuple-element.76.kv_ref, bf16[16,32,128]{2,1,0:T(8,128)(2,1)S(1)} %all-to-all-done.3.recv_ref, f32[128,128]{1,0:T(8,128)S(1)} %get-tuple-element.110.q5_ref), custom_call_target="tpu_custom_call" | custom-call | flops 2000000000 | bytes 2000000 | tf_op jit(solution)/shard_map/pallas_call | solution.py:102
  89.8 1.3 %shard_map.88 = bf16[16,48,128]{2,1,0:T(8,128)(2,1)} custom-call(s32[1]{0:T(128)} %bitcast.me_ref, bf16[128,128]{1,0:T(8,128)(2,1)S(1)} %collective-permute-done.7.beside_ref, bf16[16,64,128]{2,1,0:T(8,128)(2,1)S(1)} %all-to-all-done.4.recv_ref, f32[512,128]{1,0:T(8,128)S(1)} %get-tuple-element.111.query_ref, f32[512,128]{1,0:T(8,128)S(1)} %get-tuple-element.112.other_ref), custom_call_target="tpu_custom_call" | custom-call | flops 100000000 | bytes 2000000 | tf_op jit(solution)/shard_map/pallas_call | solution.py:102
  91.1 4.7 %all-to-all-start.5 = ((bf16[16,48,128]{2,1,0:T(8,128)(2,1)}), bf16[16,48,128]{2,1,0:T(8,128)(2,1)S(1)}, u32[]{:S(2)}, u32[]{:S(2)}) async-start(bf16[16,48,128]{2,1,0:T(8,128)(2,1)} %shard_map.88), calls=%async_computation.5 | async-start | bytes 393216 | tf_op jit(solution)/shard_map/all_to_all | solution.py:736
  95.9 6.6 %shard_map.83 = (f32[256,1024]{1,0:T(8,128)}, f32[256,1024]{1,0:T(8,128)}, f32[256,1024]{1,0:T(8,128)}) custom-call(bf16[256,1024]{1,0:T(8,128)(2,1)} %refs_0_.5, bf16[256,1024]{1,0:T(8,128)(2,1)} %refs_1_.5, bf16[256,1024]{1,0:T(8,128)(2,1)} %refs_2_.5, bf16[256,1024]{1,0:T(8,128)(2,1)} %refs_3_.1, f32[256,1024]{1,0:T(8,128)} %get-tuple-element.87.refs_4_), custom_call_target="tpu_custom_call" | custom-call | flops 8999999488 | bytes 10000000 | tf_op jit(solution)/shard_map/pallas_call | solution.py:702
  102.5 3.8 %all-to-all-done.5.refs_7_ = bf16[16,48,128]{2,1,0:T(8,128)(2,1)S(1)} async-done(((bf16[16,48,128]{2,1,0:T(8,128)(2,1)}), bf16[16,48,128]{2,1,0:T(8,128)(2,1)S(1)}, u32[]{:S(2)}, u32[]{:S(2)}) %all-to-all-start.5) | async-done | bytes 196640 | tf_op jit(solution)/shard_map/all_to_all | solution.py:736
  106.9 3.5 %shard_map.89 = (bf16[256,1024]{1,0:T(8,128)(2,1)}, bf16[256,1024]{1,0:T(8,128)(2,1)}, bf16[256,1024]{1,0:T(8,128)(2,1)}) custom-call(f32[256,1024]{1,0:T(8,128)} %get-tuple-element.88.refs_0_, f32[256,1024]{1,0:T(8,128)} %get-tuple-element.89.refs_1_, f32[256,1024]{1,0:T(8,128)} %get-tuple-element.90.refs_2_, f32[128,1024]{1,0:T(8,128)} %get-tuple-element.103.refs_3_, ...), custom_call_target="tpu_custom_call" | custom-call | flops 1000000000 | bytes 5000000 | tf_op jit(solution)/shard_map/pallas_call | solution.py:702
  (30 shorter events, 2.4 us)
Async XLA Ops:
  3.5 20.3 %all-to-all-start = ((bf16[16,48,128]{2,1,0:T(8,128)(2,1)}), bf16[16,48,128]{2,1,0:T(8,128)(2,1)S(1)}, u32[]{:S(2)}, u32[]{:S(2)}) async-start(bf16[16,48,128]{2,1,0:T(8,128)(2,1)} %get-tuple-element.60), calls=%async_computation | async-start | bytes 393216 | tf_op jit(solution)/shard_map/all_to_all | solution.py:736
  13.5 22.2 %collective-permute-start = (bf16[2,128,1024]{2,1,0:T(8,128)(2,1)}, bf16[2,128,1024]{2,1,0:T(8,128)(2,1)S(1)}, u32[]{:S(2)}, u32[]{:S(2)}) collective-permute-start(bf16[2,128,1024]{2,1,0:T(8,128)(2,1)} %get-tuple-element.69), channel_id=1, source_target_pairs={{0,1},{1,0},{2,3},{3,2},{4,5},{5,4},{6,7},{7,6},{8,9},{9,8},{10,11... | collective-permute-start | bytes 1572872 | tf_op jit(solution)/shard_map/ppermute | solution.py:739
  18.7 6.6 %copy-start.7 = (bf16[2,64,1024]{2,1,0:T(8,128)(2,1)S(1)}, bf16[2,64,1024]{2,1,0:T(8,128)(2,1)}, u32[]{:S(2)}) copy-start(bf16[2,64,1024]{2,1,0:T(8,128)(2,1)} %get-tuple-element.82) | copy-start | bytes 786436
  25.3 8.1 %collective-permute-start.2 = (bf16[2,64,1024]{2,1,0:T(8,128)(2,1)S(1)}, bf16[2,64,1024]{2,1,0:T(8,128)(2,1)S(1)}, u32[]{:S(2)}, u32[]{:S(2)}) collective-permute-start(bf16[2,64,1024]{2,1,0:T(8,128)(2,1)S(1)} %copy-done.7), channel_id=1, source_target_pairs={{0,2},{1,3},{2,0},{3,1},{4,6},{5,7},{6,4},{7,5},{8,10},{9,11},{10,... | collective-permute-start | bytes 786440 | tf_op jit(solution)/shard_map/ppermute | solution.py:739
  25.3 15.0 %all-to-all-start.1 = ((bf16[16,64,128]{2,1,0:T(8,128)(2,1)}), bf16[16,64,128]{2,1,0:T(8,128)(2,1)S(1)}, u32[]{:S(2)}, u32[]{:S(2)}) async-start(bf16[16,64,128]{2,1,0:T(8,128)(2,1)} %get-tuple-element.67), calls=%async_computation.1 | async-start | bytes 524288 | tf_op jit(solution)/shard_map/all_to_all | solution.py:736
  32.1 8.3 %collective-permute-start.1 = (bf16[128,128]{1,0:T(8,128)(2,1)S(1)}, bf16[128,128]{1,0:T(8,128)(2,1)S(1)}, u32[]{:S(2)}, u32[]{:S(2)}) collective-permute-start(bf16[128,128]{1,0:T(8,128)(2,1)S(1)} %get-tuple-element.73), channel_id=1, source_target_pairs={{0,16},{1,17},{2,18},{3,19},{4,20},{5,21},{6,22},{7,23},{8,24},{9,... | collective-permute-start | bytes 98312 | tf_op jit(solution)/shard_map/ppermute | solution.py:739
  33.5 2.2 %copy-start.6 = (bf16[2,64,1024]{2,1,0:T(8,128)(2,1)}, bf16[2,64,1024]{2,1,0:T(8,128)(2,1)S(1)}, u32[]{:S(2)}) copy-start(bf16[2,64,1024]{2,1,0:T(8,128)(2,1)S(1)} %collective-permute-done.2.refs_1_) | copy-start | bytes 786436
  33.5 13.8 %collective-permute-start.3 = (bf16[2,64,1024]{2,1,0:T(8,128)(2,1)S(1)}, bf16[2,64,1024]{2,1,0:T(8,128)(2,1)S(1)}, u32[]{:S(2)}, u32[]{:S(2)}) collective-permute-start(bf16[2,64,1024]{2,1,0:T(8,128)(2,1)S(1)} %collective-permute-done.2.refs_1_), channel_id=1, source_target_pairs={{0,1},{1,0},{2,3},{3,2},{4,5},{5,4},{6,7},{7,6},{8,9},{9,8},{10,11... | collective-permute-start | bytes 786440 | tf_op jit(solution)/shard_map/ppermute | solution.py:739
  35.7 0.8 copy-start.5
  42.3 14.2 %all-to-all-start.2 = ((bf16[16,32,128]{2,1,0:T(8,128)(2,1)}), bf16[16,32,128]{2,1,0:T(8,128)(2,1)S(1)}, u32[]{:S(2)}, u32[]{:S(2)}) async-start(bf16[16,32,128]{2,1,0:T(8,128)(2,1)} %get-tuple-element.85), calls=%async_computation.2 | async-start | bytes 262144 | tf_op jit(solution)/shard_map/all_to_all | solution.py:736
  47.3 0.7 copy-start.8
  56.5 0.7 copy-start.2
  63.0 11.9 %all-to-all-start.3 = ((bf16[16,32,128]{2,1,0:T(8,128)(2,1)}), bf16[16,32,128]{2,1,0:T(8,128)(2,1)S(1)}, u32[]{:S(2)}, u32[]{:S(2)}) async-start(bf16[16,32,128]{2,1,0:T(8,128)(2,1)} %get-tuple-element.91), calls=%async_computation.3 | async-start | bytes 262144 | tf_op jit(solution)/shard_map/all_to_all | solution.py:736
  69.9 19.1 %collective-permute-start.5 = (bf16[2,64,1024]{2,1,0:T(8,128)(2,1)}, bf16[2,64,1024]{2,1,0:T(8,128)(2,1)S(1)}, u32[]{:S(2)}, u32[]{:S(2)}) collective-permute-start(bf16[2,64,1024]{2,1,0:T(8,128)(2,1)} %get-tuple-element.107), channel_id=1, source_target_pairs={{0,1},{1,0},{2,3},{3,2},{4,5},{5,4},{6,7},{7,6},{8,9},{9,8},{10,11... | collective-permute-start | bytes 786440 | tf_op jit(solution)/shard_map/ppermute | solution.py:739
  76.8 13.1 %all-to-all-start.4 = ((bf16[16,64,128]{2,1,0:T(8,128)(2,1)}), bf16[16,64,128]{2,1,0:T(8,128)(2,1)S(1)}, u32[]{:S(2)}, u32[]{:S(2)}) async-start(bf16[16,64,128]{2,1,0:T(8,128)(2,1)} %get-tuple-element.97), calls=%async_computation.4 | async-start | bytes 524288 | tf_op jit(solution)/shard_map/all_to_all | solution.py:736
  81.3 8.6 %collective-permute-start.7 = (bf16[128,128]{1,0:T(8,128)(2,1)S(1)}, bf16[128,128]{1,0:T(8,128)(2,1)S(1)}, u32[]{:S(2)}, u32[]{:S(2)}) collective-permute-start(bf16[128,128]{1,0:T(8,128)(2,1)S(1)} %get-tuple-element.108), channel_id=1, source_target_pairs={{0,16},{1,17},{2,18},{3,19},{4,20},{5,21},{6,22},{7,23},{8,24},{9,... | collective-permute-start | bytes 98312 | tf_op jit(solution)/shard_map/ppermute | solution.py:739
  86.2 16.2 %collective-permute-start.4 = (bf16[2,128,1024]{2,1,0:T(8,128)(2,1)}, bf16[2,128,1024]{2,1,0:T(8,128)(2,1)S(1)}, u32[]{:S(2)}, u32[]{:S(2)}) collective-permute-start(bf16[2,128,1024]{2,1,0:T(8,128)(2,1)} %get-tuple-element.104), channel_id=1, source_target_pairs={{0,1},{1,0},{2,3},{3,2},{4,5},{5,4},{6,7},{7,6},{8,9},{9,8},{10,11... | collective-permute-start | bytes 1572872 | tf_op jit(solution)/shard_map/ppermute | solution.py:739
  87.0 1.9 %copy-start.3 = (f32[2,64,1024]{2,1,0:T(8,128)S(1)}, f32[2,64,1024]{2,1,0:T(8,128)}, u32[]{:S(2)}) copy-start(f32[2,64,1024]{2,1,0:T(8,128)} %get-tuple-element.106) | copy-start | bytes 1572868
  89.0 13.4 %collective-permute-start.6 = (bf16[2,64,1024]{2,1,0:T(8,128)(2,1)S(1)}, bf16[2,64,1024]{2,1,0:T(8,128)(2,1)S(1)}, u32[]{:S(2)}, u32[]{:S(2)}) collective-permute-start(bf16[2,64,1024]{2,1,0:T(8,128)(2,1)S(1)} %add_convert_fusion), channel_id=1, source_target_pairs={{0,2},{1,3},{2,0},{3,1},{4,6},{5,7},{6,4},{7,5},{8,10},{9,11},{10,... | collective-permute-start | bytes 786440 | tf_op jit(solution)/shard_map/ppermute | solution.py:739
  91.1 15.1 %all-to-all-start.5 = ((bf16[16,48,128]{2,1,0:T(8,128)(2,1)}), bf16[16,48,128]{2,1,0:T(8,128)(2,1)S(1)}, u32[]{:S(2)}, u32[]{:S(2)}) async-start(bf16[16,48,128]{2,1,0:T(8,128)(2,1)} %shard_map.88), calls=%async_computation.5 | async-start | bytes 393216 | tf_op jit(solution)/shard_map/all_to_all | solution.py:736
  102.4 3.8 %copy-start.4 = (bf16[2,64,1024]{2,1,0:T(8,128)(2,1)}, bf16[2,64,1024]{2,1,0:T(8,128)(2,1)S(1)}, u32[]{:S(2)}) copy-start(bf16[2,64,1024]{2,1,0:T(8,128)(2,1)S(1)} %collective-permute-done.6.refs_6_) | copy-start | bytes 786436
  102.5 3.8 %copy-start.1 = (bf16[2,128,1024]{2,1,0:T(8,128)(2,1)}, bf16[2,128,1024]{2,1,0:T(8,128)(2,1)S(1)}, u32[]{:S(2)}) copy-start(bf16[2,128,1024]{2,1,0:T(8,128)(2,1)S(1)} %collective-permute-done.4.refs_4_) | copy-start | bytes 1572868
  106.3 0.7 copy-start
where the time goes:
time: 111 us
  Pallas kernels  46.5 us (42%)
  starting transfers between devices  39.6 us (36%)
  waiting for transfers between devices  20.7 us (19%)
  local copies, waits for them, and re-layouts  2.83 us (3%)
    pallas_call x9, Pallas kernels, over_pairs(): pl.pallas_call(body, grid=(PAIRS // step,), out_shape=[jax.ShapeDtypeStru...  36.8 us
    all_to_all x6, starting transfers between devices, exchange(): return lax.all_to_all(x, 'seq', 0, 0, axis_index_groups=groups, tiled=True)  34.4 us
    all_to_all x6, waiting for transfers between devices, exchange(): return lax.all_to_all(x, 'seq', 0, 0, axis_index_groups=groups, tiled=True)  20.7 us
    pallas_call x6, Pallas kernels, call(): pl.pallas_call(kernel, out_shape=[jax.ShapeDtypeStruct(s, d) for s, d in...  9.65 us
    ppermute x8, starting transfers between devices, swapped(): return lax.ppermute(x, 'seq', pairs_of(mask, size))  5.16 us
    unnamed x18, local copies, waits for them, and re-layouts  2.83 us
  transfers between devices with their start and end apart: 14, of which 6 were waited for; matrix products, arithmetic and copies ran while one was open for 0% of the time, Pallas kernels for 31%

commit v1 on v0

--- a/solution.py
+++ b/solution.py
@@ -123,6 +123,7 @@
     low16 = low_lanes(16)
     level3 = []
     for index, ref in enumerate((q_ref, k_ref, v_ref)):
+        yield
         one = halved(one_s.at[index], ref[...].astype(F32))
         two = halved(two_s.at[index], one.astype(F32))
         if index == 0:
@@ -213,14 +214,14 @@
 def own_forward_kernel(steps):
     pairs = [(q[...], k[...], v[...]) for q, k, v, _, _ in steps]
     for views, (att, lse) in zip(steps, heads_forward(pairs, 0.0)):
-        views[3][...] = att
+        views[3][...] = att.astype(BF16)
         views[4][...] = lse
 
 
 def core_forward_kernel(steps):
     pairs = [(q[...], kv[0], kv[1]) for q, kv, _, _ in steps]
     for views, (att, lse) in zip(steps, heads_forward(pairs, LN2)):
-        views[2][...] = att
+        views[2][...] = att.astype(BF16)
         views[3][...] = lse
 
 
@@ -234,7 +235,7 @@
 def ring_forward_kernel(steps):
     pairs = [(q[...],) + ring_pair(kva, kvb) for q, kva, kvb, _, _ in steps]
     for views, (att, lse) in zip(steps, heads_forward(pairs, 2.0 * LN2)):
-        views[3][...] = att
+        views[3][...] = att.astype(BF16)
         views[4][...] = lse
 
 
@@ -359,6 +360,7 @@
         columns.append(jnp.sum(jnp.where(own, line, 0.0), axis=1, keepdims=True))
     lse = jnp.where(low_lanes(32), columns[0], columns[1])
     att = att3
+    yield
     for index, (att_ref, lse_ref) in enumerate(
         ((att2_ref, lse2_ref), (att1_ref, lse1_ref), (att0_ref, lse0_ref))
     ):
@@ -369,17 +371,19 @@
         e_up = jnp.exp(lse - high)
         e_own = jnp.exp(own_lse - high)
         den = e_up + e_own
-        att = (e_up * att + e_own * att_ref[...]) / den
+        att = (e_up * att + e_own * att_ref[...].astype(F32)) / den
         lse = high + jnp.log(den)
+        yield
     attended = att.astype(BF16)
     full = lse
     out_ref[...] = attended
     grad = grad_ref[...].astype(F32)
     product = grad * attended.astype(F32)
     align = None
-    for part in pieces(product, 3):
+    for part in pieces(product, 2):
         term = dot(part, per_head)
         align = term if align is None else align + term
+    yield
     stat_ref[...] = jnp.where(lane_of(256) & 32 == 0, full, align)
     lse_s[...] = full
     grad_s[...] = grad
@@ -399,12 +403,14 @@
     r1, g1, f1 = fold(lse_s, grad_s, align_s, 128)
     stat1_ref[...] = jnp.where(lane_of(B) & 32 == 0, r1, f1)
     g1_ref[...] = g1.astype(BF16)
+    yield
     r_s[...] = r1
     g_s[...] = g1
     f_s[...] = f1
     r2, g2, f2 = fold(r_s, g_s, f_s, 64)
     stat2_ref[...] = jnp.where(lane_of(64) & 32 == 0, r2, f2)
     g2_ref[...] = g2.astype(BF16)
+    yield
     r2_s[...] = r2
     g2_s[...] = g2
     f2_s[...] = f2
@@ -413,6 +419,7 @@
     diagonal = row32 == (lane_of(32) & (E - 1))
     line_r = place(r3, diagonal)
     line_f = place(f3, diagonal)
+    yield
     low1 = low_lanes(1)
     wide_r = jnp.broadcast_to(line_r, (8, LANES))
     wide_f = jnp.broadcast_to(line_f, (8, LANES))
@@ -601,13 +608,13 @@
     pairs = [tuple(view[...] for view in views[:5]) for views in steps]
     for views, grads in zip(steps, heads_backward(pairs, 0.0)):
         for view, value in zip(views[5:], grads):
-            view[...] = value
+            view[...] = value.astype(BF16)
 
 
 def core_backward_kernel(steps):
     pairs = [(q[...], kv[0], kv[1], g[...], stat[...]) for q, kv, stat, g, _, _ in steps]
     for views, (dq, dk, dv) in zip(steps, heads_backward(pairs, LN2)):
-        views[4][...] = dq
+        views[4][...] = dq.astype(BF16)
         views[5][0] = dk.astype(BF16)
         views[5][1] = dv.astype(BF16)
 
@@ -618,7 +625,7 @@
         for views in steps
     ]
     for views, (dq, dk, dv) in zip(steps, heads_backward(pairs, 2.0 * LN2)):
-        views[5][...] = dq
+        views[5][...] = dq.astype(BF16)
         views[6][0] = dk[0:64]
         views[6][1] = dv[0:64]
         views[7][0] = dk[64:128].astype(BF16)
@@ -644,18 +651,25 @@
         axis=0,
     )
     work = (
-        (dq_ref, dq1_ref[...], dq2_ref[...], g3q, q_out),
+        (dq_ref, dq1_ref[...].astype(F32), dq2_ref[...].astype(F32), g3q, q_out),
         (dk_ref, kv1_ref[0].astype(F32), kv2_ref[0].astype(F32), g3k, k_out),
         (dv_ref, kv1_ref[1].astype(F32), kv2_ref[1].astype(F32), g3v, v_out),
     )
     for index, (own, one, two, three, out) in enumerate(work):
+        yield
         two = two + repeated(quarter_s.at[index], three * 0.5, 2)
         one = one + repeated(half_s.at[index], two * 0.5, 2)
-        out[...] = (own[...] + repeated(full_s.at[index], one * 0.5, 2)).astype(BF16)
+        out[...] = (own[...].astype(F32) + repeated(full_s.at[index], one * 0.5, 2)).astype(BF16)
 
 
 def pairs_of(mask, size):
     return [(source, source ^ mask) for source in range(size)]
+
+
+def in_turn(kernel, steps):
+    running = [kernel(*views) for views in steps]
+    while running:
+        running = [g for g in running if next(g, 0) is None]
 
 
 class Tall:
@@ -692,12 +706,15 @@
     kinds = in_kinds + out_kinds
 
     def body(*refs):
+        steps = [
+            [kind.view(ref, i) for kind, ref in zip(kinds, refs)]
+            + [ref.at[i] for ref in refs[len(kinds) :]]
+            for i in range(step)
+        ]
         if joint:
-            kernel([[kind.view(ref, i) for kind, ref in zip(kinds, refs)] for i in range(step)])
-            return
-        for i in range(step):
-            views = [kind.view(ref, i) for kind, ref in zip(kinds, refs)]
-            kernel(*views, *[ref.at[i] for ref in refs[len(kinds) :]])
+            kernel(steps)
+        else:
+            in_turn(kernel, steps)
 
     return pl.pallas_call(
         body,
@@ -706,22 +723,14 @@
         in_specs=[kind.spec(step) for kind in in_kinds],
         out_specs=[kind.spec(step) for kind in out_kinds],
         scratch_shapes=[pltpu.VMEM((step,) + shape + (LANES,), F32) for shape in scratch],
-        compiler_params=pltpu.CompilerParams(vmem_limit_bytes=58 * 1024 * 1024),
+        compiler_params=pltpu.CompilerParams(vmem_limit_bytes=STEPS["limit"] * 1024 * 1024),
         cost_estimate=pl.CostEstimate(
             flops=int(flops), bytes_accessed=int(moved), transcendentals=0
         ),
     )(*ins)
 
 
-STEPS = {
-    "pool": 4,
-    "local_forward": 2,
-    "combine": 4,
-    "local_backward": 2,
-    "final": 4,
-    "core_forward": 4,
-    "core_backward": 4,
-}
+STEPS = {"pool": 4, "local_forward": 4, "combine": 4, "local_backward": 4, "final": 4, "core_forward": 8, "core_backward": 4, "limit": 60}
 
 
 def per_device(q, k, v, grad):
@@ -759,7 +768,7 @@
     full = ((rows, width), F32)
     att0, lse0 = over_pairs(
         own_forward_kernel,
-        [full, full],
+        [((rows, width), BF16), full],
         [Tall(rows)] * 2,
         (q, k, v),
         [Tall(rows)] * 3,
@@ -783,7 +792,7 @@
     half = (B, width)
     att1, lse1 = over_pairs(
         core_forward_kernel,
-        [(half, F32)] * 2,
+        [(half, BF16), (half, F32)],
         [Tall(B)] * 2,
         (q1, kv1s),
         [Tall(B), TwoTall(B)],
@@ -805,7 +814,7 @@
     recv2 = exchange(send2, rings)
     att2, lse2 = over_pairs(
         ring_forward_kernel,
-        [(quarter, F32)] * 2,
+        [(quarter, BF16), (quarter, F32)],
         [Tall(64)] * 2,
         (q2_later, kv2a, kv2b),
         [Tall(64), TwoTall(64), TwoTall(64)],
@@ -833,7 +842,7 @@
     recv3 = exchange(send3, rings)
     dq2, same, across = over_pairs(
         ring_backward_kernel,
-        [(quarter, F32), ((2,) + quarter, F32), ((2,) + quarter, BF16)],
+        [(quarter, BF16), ((2,) + quarter, F32), ((2,) + quarter, BF16)],
         [Tall(64), TwoTall(64), TwoTall(64)],
         (q2, kv2a, kv2b, stat2, g2),
         [Tall(64), TwoTall(64), TwoTall(64), Tall(64), Tall(64)],
@@ -864,7 +873,7 @@
     )
     dq1, dkv1 = over_pairs(
         core_backward_kernel,
-        [(half, F32), ((2, B, width), BF16)],
+        [(half, BF16), ((2, B, width), BF16)],
         [Tall(B), TwoTall(B)],
         (q1_late, kv1s, stat1, g1),
         [Tall(B), TwoTall(B)] + [Tall(B)] * 2,
@@ -883,7 +892,7 @@
     recv4 = exchange(send4, rings)
     dq, dk, dv = over_pairs(
         own_backward_kernel,
-        [full] * 3,
+        [((rows, width), BF16)] * 3,
         [Tall(rows)] * 3,
         (q, k, v, grad, stat),
         [Tall(rows)] * 5,

time: 111 us -> 110 us (level)
  Pallas kernels: 46.5 us -> 43.2 us
  waiting for transfers between devices: 20.7 us -> 23.1 us
    pallas_call x9, Pallas kernels: 36.8 us -> 33.6 us  [over_pairs(): pl.pallas_call(body, grid=(PAIRS // step,), out_shape=[jax.ShapeDtypeStru...]
    all_to_all x6, waiting for transfers between devices: 20.7 us -> 23.1 us  [exchange(): return lax.all_to_all(x, 'seq', 0, 0, axis_index_groups=groups, tiled=True)]
  transfers between devices with their start and end apart: 14 -> 14, of which waited for: 6 -> 6; matrix products, arithmetic and copies ran while one was open for 0% -> 0% of each run, Pallas kernels for 31% -> 29%
where the time goes in v1:
time: 110 us; the launch traced here: 109 us
  Pallas kernels  43.2 us (39%)
  starting transfers between devices  39.4 us (36%)
  waiting for transfers between devices  23.1 us (21%)
  local copies, waits for them, and re-layouts  2.87 us (3%)
    all_to_all x6, starting transfers between devices, exchange(): return lax.all_to_all(x, 'seq', 0, 0, axis_index_groups=groups, tiled=True)  34.2 us
    pallas_call x9, Pallas kernels, over_pairs(): pl.pallas_call(body, grid=(PAIRS // step,), out_shape=[jax.ShapeDtypeStru...  33.6 us
    all_to_all x6, waiting for transfers between devices, exchange(): return lax.all_to_all(x, 'seq', 0, 0, axis_index_groups=groups, tiled=True)  23.1 us
    pallas_call x6, Pallas kernels, call(): pl.pallas_call(kernel, out_shape=[jax.ShapeDtypeStruct(s, d) for s, d in...  9.65 us
    ppermute x8, starting transfers between devices, swapped(): return lax.ppermute(x, 'seq', pairs_of(mask, size))  5.17 us
    unnamed x18, local copies, waits for them, and re-layouts  2.87 us
  transfers between devices with their start and end apart: 14, of which 6 were waited for; matrix products, arithmetic and copies ran while one was open for 0% of the time, Pallas kernels for 29%

profile of v1, /device:TPU:1, one launch (start us, length us, event | category | flops | bytes accessed | tf_op | source)
XLA Modules:
  0.0 109.5 jit_solution(7219629277400860731)
XLA Ops:
  0.6 2.9 %shard_map.75 = (bf16[128,1024]{1,0:T(8,128)(2,1)}, bf16[2,128,1024]{2,1,0:T(8,128)(2,1)}, bf16[64,1024]{1,0:T(8,128)(2,1)}, bf16[2,64,1024]{2,1,0:T(8,128)(2,1)}, bf16[16,48,128]{2,1,0:T(8,128)(2,1)}) custom-call(bf16[256,1024]{1,0:T(8,128)(2,1)} %refs_0_.5, bf16[256,1024]{1,0:T(8,128)(2,1)} %refs_1_.5, bf16[256,1024]{1,0:T(8,128)(2,1)} %refs_2_.5), custom_call_target="tpu_custom_call" | custom-call | flops 1000000000 | bytes 5000000 | tf_op jit(solution)/shard_map/pallas_call | solution.py:719
  3.5 10.0 %all-to-all-start = ((bf16[16,48,128]{2,1,0:T(8,128)(2,1)}), bf16[16,48,128]{2,1,0:T(8,128)(2,1)S(1)}, u32[]{:S(2)}, u32[]{:S(2)}) async-start(bf16[16,48,128]{2,1,0:T(8,128)(2,1)} %get-tuple-element.60), calls=%async_computation | async-start | bytes 393216 | tf_op jit(solution)/shard_map/all_to_all | solution.py:745
  13.7 4.0 %shard_map.76 = (bf16[256,1024]{1,0:T(8,128)(2,1)}, f32[256,1024]{1,0:T(8,128)}) custom-call(bf16[256,1024]{1,0:T(8,128)(2,1)} %refs_0_.5, bf16[256,1024]{1,0:T(8,128)(2,1)} %refs_1_.5, bf16[256,1024]{1,0:T(8,128)(2,1)} %refs_2_.5), custom_call_target="tpu_custom_call" | custom-call | flops 6000000000 | bytes 10000000 | tf_op jit(solution)/shard_map/pallas_call | solution.py:719
  17.7 6.2 %all-to-all-done.recv_ref = bf16[16,48,128]{2,1,0:T(8,128)(2,1)S(1)} async-done(((bf16[16,48,128]{2,1,0:T(8,128)(2,1)}), bf16[16,48,128]{2,1,0:T(8,128)(2,1)S(1)}, u32[]{:S(2)}, u32[]{:S(2)}) %all-to-all-start) | async-done | bytes 196640 | tf_op jit(solution)/shard_map/all_to_all | solution.py:745
  23.8 1.5 %shard_map.77 = (bf16[1024,128]{1,0:T(8,128)(2,1)S(1)}, bf16[1024,128]{1,0:T(8,128)(2,1)S(1)}, bf16[128,128]{1,0:T(8,128)(2,1)S(1)}, bf16[16,64,128]{2,1,0:T(8,128)(2,1)}) custom-call(s32[1]{0:T(128)} %bitcast.me_ref, bf16[16,48,128]{2,1,0:T(8,128)(2,1)S(1)} %all-to-all-done.recv_ref), custom_call_target="tpu_custom_call" | custom-call | flops 100000000 | bytes 2000000 | tf_op jit(solution)/shard_map/pallas_call | solution.py:102
  25.3 6.8 %all-to-all-start.1 = ((bf16[16,64,128]{2,1,0:T(8,128)(2,1)}), bf16[16,64,128]{2,1,0:T(8,128)(2,1)S(1)}, u32[]{:S(2)}, u32[]{:S(2)}) async-start(bf16[16,64,128]{2,1,0:T(8,128)(2,1)} %get-tuple-element.67), calls=%async_computation.1 | async-start | bytes 524288 | tf_op jit(solution)/shard_map/all_to_all | solution.py:745
  32.1 1.4 %collective-permute-start.1 = (bf16[128,128]{1,0:T(8,128)(2,1)S(1)}, bf16[128,128]{1,0:T(8,128)(2,1)S(1)}, u32[]{:S(2)}, u32[]{:S(2)}) collective-permute-start(bf16[128,128]{1,0:T(8,128)(2,1)S(1)} %get-tuple-element.73), channel_id=1, source_target_pairs={{0,16},{1,17},{2,18},{3,19},{4,20},{5,21},{6,22},{7,23},{8,24},{9,... | collective-permute-start | bytes 98312 | tf_op jit(solution)/shard_map/ppermute | solution.py:748
  33.5 1.1 collective-permute-start.3
  34.5 1.1 %shard_map.79 = (f32[512,128]{1,0:T(8,128)S(1)}, f32[512,128]{1,0:T(8,128)S(1)}) custom-call(bf16[1024,128]{1,0:T(8,128)(2,1)S(1)} %get-tuple-element.75.q_ref, bf16[1024,128]{1,0:T(8,128)(2,1)S(1)} %get-tuple-element.76.kv_ref), custom_call_target="tpu_custom_call" | custom-call | flops 1000000000 | bytes 2000000 | tf_op jit(solution)/shard_map/pallas_call | solution.py:102
  35.7 0.8 copy-done.3
  36.5 2.8 %shard_map.78 = (bf16[128,1024]{1,0:T(8,128)(2,1)}, f32[128,1024]{1,0:T(8,128)}) custom-call(bf16[128,1024]{1,0:T(8,128)(2,1)} %get-tuple-element.99.refs_0_, bf16[2,128,1024]{2,1,0:T(8,128)(2,1)} %copy-done.3), custom_call_target="tpu_custom_call" | custom-call | flops 2000000000 | bytes 5000000 | tf_op jit(solution)/shard_map/pallas_call | solution.py:719
  39.3 1.1 all-to-all-done.1.recv_ref
  40.4 1.9 %shard_map.80 = (bf16[16,32,128]{2,1,0:T(8,128)(2,1)}, bf16[4,128,128]{2,1,0:T(8,128)(2,1)S(1)}) custom-call(s32[1]{0:T(128)} %bitcast.me_ref, bf16[128,128]{1,0:T(8,128)(2,1)S(1)} %collective-permute-done.1.beside_ref, bf16[16,64,128]{2,1,0:T(8,128)(2,1)S(1)} %all-to-all-done.1.recv_ref, bf16[1024,128]{1,0:T(8,128)(2,1)S(1)} %get-tuple-element.75.q_ref, ...), custom_call_target="tpu_custom_call" | custom-call | flops 100000000 | bytes 2000000 | tf_op jit(solution)/shard_map/pallas_call | solution.py:102
  42.3 5.0 %all-to-all-start.2 = ((bf16[16,32,128]{2,1,0:T(8,128)(2,1)}), bf16[16,32,128]{2,1,0:T(8,128)(2,1)S(1)}, u32[]{:S(2)}, u32[]{:S(2)}) async-start(bf16[16,32,128]{2,1,0:T(8,128)(2,1)} %get-tuple-element.85), calls=%async_computation.2 | async-start | bytes 262144 | tf_op jit(solution)/shard_map/all_to_all | solution.py:745
  47.3 0.7 copy-done.7
  48.0 2.7 %shard_map.81 = (bf16[64,1024]{1,0:T(8,128)(2,1)}, f32[64,1024]{1,0:T(8,128)}) custom-call(bf16[64,1024]{1,0:T(8,128)(2,1)} %get-tuple-element.81.refs_0_, bf16[2,64,1024]{2,1,0:T(8,128)(2,1)} %copy-done.5, bf16[2,64,1024]{2,1,0:T(8,128)(2,1)} %copy-done.7), custom_call_target="tpu_custom_call" | custom-call | flops 2000000000 | bytes 5000000 | tf_op jit(solution)/shard_map/pallas_call | solution.py:719
  50.7 5.8 %all-to-all-done.2.refs_6_ = bf16[16,32,128]{2,1,0:T(8,128)(2,1)S(1)} async-done(((bf16[16,32,128]{2,1,0:T(8,128)(2,1)}), bf16[16,32,128]{2,1,0:T(8,128)(2,1)S(1)}, u32[]{:S(2)}, u32[]{:S(2)}) %all-to-all-start.2) | async-done | bytes 131104 | tf_op jit(solution)/shard_map/all_to_all | solution.py:745
  57.2 5.4 %shard_map.82 = (bf16[256,1024]{1,0:T(8,128)(2,1)}, f32[256,1024]{1,0:T(8,128)}, f32[128,1024]{1,0:T(8,128)}, bf16[128,1024]{1,0:T(8,128)(2,1)}, f32[64,1024]{1,...) custom-call(bf16[256,1024]{1,0:T(8,128)(2,1)} %get-tuple-element.62.refs_0_, ...), custom_call_target="tpu_custom_call" | custom-call | flops 1000000000 | bytes 5000000 | tf_op jit(solution)/shard_map/pallas_call | solution.py:719
  62.6 3.4 %all-to-all-start.3 = ((bf16[16,32,128]{2,1,0:T(8,128)(2,1)}), bf16[16,32,128]{2,1,0:T(8,128)(2,1)S(1)}, u32[]{:S(2)}, u32[]{:S(2)}) async-start(bf16[16,32,128]{2,1,0:T(8,128)(2,1)} %get-tuple-element.91), calls=%async_computation.3 | async-start | bytes 262144 | tf_op jit(solution)/shard_map/all_to_all | solution.py:745
  66.0 3.5 %shard_map.84 = (bf16[64,1024]{1,0:T(8,128)(2,1)}, f32[2,64,1024]{2,1,0:T(8,128)}, bf16[2,64,1024]{2,1,0:T(8,128)(2,1)}) custom-call(bf16[64,1024]{1,0:T(8,128)(2,1)} %get-tuple-element.81.refs_0_, bf16[2,64,1024]{2,1,0:T(8,128)(2,1)} %copy-done.5, bf16[2,64,1024]{2,1,0:T(8,128)(2,1)} %copy-done.7, f32[64,1024]{1,0:T(8,128)} %get-tuple-element.92.refs_3_, ...), custom_call_target="tpu_custom_call" | custom-call | flops 3000000000 | bytes 5000000 | tf_op jit(solution)/shard_map/pallas_call | solution.py:719
  69.5 5.0 %all-to-all-done.3.recv_ref = bf16[16,32,128]{2,1,0:T(8,128)(2,1)S(1)} async-done(((bf16[16,32,128]{2,1,0:T(8,128)(2,1)}), bf16[16,32,128]{2,1,0:T(8,128)(2,1)S(1)}, u32[]{:S(2)}, u32[]{:S(2)}) %all-to-all-start.3) | async-done | bytes 131104 | tf_op jit(solution)/shard_map/all_to_all | solution.py:745
  74.5 1.9 %shard_map.85 = (f32[128,128]{1,0:T(8,128)S(1)}, bf16[128,128]{1,0:T(8,128)(2,1)S(1)}, bf16[16,64,128]{2,1,0:T(8,128)(2,1)}) custom-call(s32[1]{0:T(128)} %bitcast.me_ref, bf16[16,32,128]{2,1,0:T(8,128)(2,1)S(1)} %all-to-all-done.3.recv_ref, bf16[1024,128]{1,0:T(8,128)(2,1)S(1)} %get-tuple-element.75.q_ref, ...), custom_call_target="tpu_custom_call" | custom-call | flops 100000000 | bytes 2000000 | tf_op jit(solution)/shard_map/pallas_call | solution.py:102
  76.4 4.3 %all-to-all-start.4 = ((bf16[16,64,128]{2,1,0:T(8,128)(2,1)}), bf16[16,64,128]{2,1,0:T(8,128)(2,1)S(1)}, u32[]{:S(2)}, u32[]{:S(2)}) async-start(bf16[16,64,128]{2,1,0:T(8,128)(2,1)} %get-tuple-element.97), calls=%async_computation.4 | async-start | bytes 524288 | tf_op jit(solution)/shard_map/all_to_all | solution.py:745
  80.6 1.4 %collective-permute-start.7 = (bf16[128,128]{1,0:T(8,128)(2,1)S(1)}, bf16[128,128]{1,0:T(8,128)(2,1)S(1)}, u32[]{:S(2)}, u32[]{:S(2)}) collective-permute-start(bf16[128,128]{1,0:T(8,128)(2,1)S(1)} %get-tuple-element.108), channel_id=1, source_target_pairs={{0,16},{1,17},{2,18},{3,19},{4,20},{5,21},{6,22},{7,23},{8,24},{9,... | collective-permute-start | bytes 98312 | tf_op jit(solution)/shard_map/ppermute | solution.py:748
  82.0 3.6 %shard_map.86 = (bf16[128,1024]{1,0:T(8,128)(2,1)}, bf16[2,128,1024]{2,1,0:T(8,128)(2,1)}) custom-call(bf16[128,1024]{1,0:T(8,128)(2,1)} %get-tuple-element.99.refs_0_, bf16[2,128,1024]{2,1,0:T(8,128)(2,1)} %copy-done.3, f32[128,1024]{1,0:T(8,128)} %get-tuple-element.100.refs_2_, bf16[128,1024]{1,0:T(8,128)(2,1)} %get-tuple-element.101.refs_3_), custom_call_target="tpu_custom_call" | custom-call | flops 3000000000 | bytes 5000000 | tf_op jit(solution)/shard_map/pallas_call | solution.py:719
  85.5 0.8 collective-permute-start.4
  86.4 1.9 %shard_map.87 = (f32[512,128]{1,0:T(8,128)S(1)}, f32[512,128]{1,0:T(8,128)S(1)}) custom-call(bf16[1024,128]{1,0:T(8,128)(2,1)S(1)} %get-tuple-element.75.q_ref, bf16[1024,128]{1,0:T(8,128)(2,1)S(1)} %get-tuple-element.76.kv_ref, bf16[16,32,128]{2,1,0:T(8,128)(2,1)S(1)} %all-to-all-done.3.recv_ref, f32[128,128]{1,0:T(8,128)S(1)} %get-tuple-element.110.q5_ref), custom_call_target="tpu_custom_call" | custom-call | flops 2000000000 | bytes 2000000 | tf_op jit(solution)/shard_map/pallas_call | solution.py:102
  89.2 1.3 %shard_map.88 = bf16[16,48,128]{2,1,0:T(8,128)(2,1)} custom-call(s32[1]{0:T(128)} %bitcast.me_ref, bf16[128,128]{1,0:T(8,128)(2,1)S(1)} %collective-permute-done.7.beside_ref, bf16[16,64,128]{2,1,0:T(8,128)(2,1)S(1)} %all-to-all-done.4.recv_ref, f32[512,128]{1,0:T(8,128)S(1)} %get-tuple-element.111.query_ref, f32[512,128]{1,0:T(8,128)S(1)} %get-tuple-element.112.other_ref), custom_call_target="tpu_custom_call" | custom-call | flops 100000000 | bytes 2000000 | tf_op jit(solution)/shard_map/pallas_call | solution.py:102
  90.5 4.7 %all-to-all-start.5 = ((bf16[16,48,128]{2,1,0:T(8,128)(2,1)}), bf16[16,48,128]{2,1,0:T(8,128)(2,1)S(1)}, u32[]{:S(2)}, u32[]{:S(2)}) async-start(bf16[16,48,128]{2,1,0:T(8,128)(2,1)} %shard_map.88), calls=%async_computation.5 | async-start | bytes 393216 | tf_op jit(solution)/shard_map/all_to_all | solution.py:745
  95.3 5.8 %shard_map.83 = (bf16[256,1024]{1,0:T(8,128)(2,1)}, bf16[256,1024]{1,0:T(8,128)(2,1)}, bf16[256,1024]{1,0:T(8,128)(2,1)}) custom-call(bf16[256,1024]{1,0:T(8,128)(2,1)} %refs_0_.5, bf16[256,1024]{1,0:T(8,128)(2,1)} %refs_1_.5, bf16[256,1024]{1,0:T(8,128)(2,1)} %refs_2_.5, bf16[256,1024]{1,0:T(8,128)(2,1)} %refs_3_.1, f32[256,1024]{1,0:T(8,128)} %get-tuple-element.87.refs_4_), custom_call_target="tpu_custom_call" | custom-call | flops 8999999488 | bytes 10000000 | tf_op jit(solution)/shard_map/pallas_call | solution.py:719
  101.0 4.6 %all-to-all-done.5.refs_7_ = bf16[16,48,128]{2,1,0:T(8,128)(2,1)S(1)} async-done(((bf16[16,48,128]{2,1,0:T(8,128)(2,1)}), bf16[16,48,128]{2,1,0:T(8,128)(2,1)S(1)}, u32[]{:S(2)}, u32[]{:S(2)}) %all-to-all-start.5) | async-done | bytes 196640 | tf_op jit(solution)/shard_map/all_to_all | solution.py:745
  106.3 3.1 %shard_map.89 = (bf16[256,1024]{1,0:T(8,128)(2,1)}, bf16[256,1024]{1,0:T(8,128)(2,1)}, bf16[256,1024]{1,0:T(8,128)(2,1)}) custom-call(bf16[256,1024]{1,0:T(8,128)(2,1)} %get-tuple-element.88.refs_0_, bf16[256,1024]{1,0:T(8,128)(2,1)} %get-tuple-element.89.refs_1_, bf16[256,1024]{1,0:T(8,128)(2,1)} %get-tuple-element.90.refs_2_, ...), custom_call_target="tpu_custom_call" | custom-call | flops 1000000000 | bytes 5000000 | tf_op jit(solution)/shard_map/pallas_call | solution.py:719
  (30 shorter events, 2.5 us)
Async XLA Ops:
  3.5 20.3 %all-to-all-start = ((bf16[16,48,128]{2,1,0:T(8,128)(2,1)}), bf16[16,48,128]{2,1,0:T(8,128)(2,1)S(1)}, u32[]{:S(2)}, u32[]{:S(2)}) async-start(bf16[16,48,128]{2,1,0:T(8,128)(2,1)} %get-tuple-element.60), calls=%async_computation | async-start | bytes 393216 | tf_op jit(solution)/shard_map/all_to_all | solution.py:745
  13.5 22.2 %collective-permute-start = (bf16[2,128,1024]{2,1,0:T(8,128)(2,1)}, bf16[2,128,1024]{2,1,0:T(8,128)(2,1)S(1)}, u32[]{:S(2)}, u32[]{:S(2)}) collective-permute-start(bf16[2,128,1024]{2,1,0:T(8,128)(2,1)} %get-tuple-element.69), channel_id=1, source_target_pairs={{0,1},{1,0},{2,3},{3,2},{4,5},{5,4},{6,7},{7,6},{8,9},{9,8},{10,11... | collective-permute-start | bytes 1572872 | tf_op jit(solution)/shard_map/ppermute | solution.py:748
  17.7 7.7 %copy-start.6 = (bf16[2,64,1024]{2,1,0:T(8,128)(2,1)S(1)}, bf16[2,64,1024]{2,1,0:T(8,128)(2,1)}, u32[]{:S(2)}) copy-start(bf16[2,64,1024]{2,1,0:T(8,128)(2,1)} %get-tuple-element.82) | copy-start | bytes 786436
  25.3 8.1 %collective-permute-start.2 = (bf16[2,64,1024]{2,1,0:T(8,128)(2,1)S(1)}, bf16[2,64,1024]{2,1,0:T(8,128)(2,1)S(1)}, u32[]{:S(2)}, u32[]{:S(2)}) collective-permute-start(bf16[2,64,1024]{2,1,0:T(8,128)(2,1)S(1)} %copy-done.6), channel_id=1, source_target_pairs={{0,2},{1,3},{2,0},{3,1},{4,6},{5,7},{6,4},{7,5},{8,10},{9,11},{10,... | collective-permute-start | bytes 786440 | tf_op jit(solution)/shard_map/ppermute | solution.py:748
  25.3 15.0 %all-to-all-start.1 = ((bf16[16,64,128]{2,1,0:T(8,128)(2,1)}), bf16[16,64,128]{2,1,0:T(8,128)(2,1)S(1)}, u32[]{:S(2)}, u32[]{:S(2)}) async-start(bf16[16,64,128]{2,1,0:T(8,128)(2,1)} %get-tuple-element.67), calls=%async_computation.1 | async-start | bytes 524288 | tf_op jit(solution)/shard_map/all_to_all | solution.py:745
  32.1 8.3 %collective-permute-start.1 = (bf16[128,128]{1,0:T(8,128)(2,1)S(1)}, bf16[128,128]{1,0:T(8,128)(2,1)S(1)}, u32[]{:S(2)}, u32[]{:S(2)}) collective-permute-start(bf16[128,128]{1,0:T(8,128)(2,1)S(1)} %get-tuple-element.73), channel_id=1, source_target_pairs={{0,16},{1,17},{2,18},{3,19},{4,20},{5,21},{6,22},{7,23},{8,24},{9,... | collective-permute-start | bytes 98312 | tf_op jit(solution)/shard_map/ppermute | solution.py:748
  33.5 2.2 %copy-start.5 = (bf16[2,64,1024]{2,1,0:T(8,128)(2,1)}, bf16[2,64,1024]{2,1,0:T(8,128)(2,1)S(1)}, u32[]{:S(2)}) copy-start(bf16[2,64,1024]{2,1,0:T(8,128)(2,1)S(1)} %collective-permute-done.2.refs_1_) | copy-start | bytes 786436
  33.5 13.8 %collective-permute-start.3 = (bf16[2,64,1024]{2,1,0:T(8,128)(2,1)S(1)}, bf16[2,64,1024]{2,1,0:T(8,128)(2,1)S(1)}, u32[]{:S(2)}, u32[]{:S(2)}) collective-permute-start(bf16[2,64,1024]{2,1,0:T(8,128)(2,1)S(1)} %collective-permute-done.2.refs_1_), channel_id=1, source_target_pairs={{0,1},{1,0},{2,3},{3,2},{4,5},{5,4},{6,7},{7,6},{8,9},{9,8},{10,11... | collective-permute-start | bytes 786440 | tf_op jit(solution)/shard_map/ppermute | solution.py:748
  35.7 0.8 copy-start.3
  42.3 14.2 %all-to-all-start.2 = ((bf16[16,32,128]{2,1,0:T(8,128)(2,1)}), bf16[16,32,128]{2,1,0:T(8,128)(2,1)S(1)}, u32[]{:S(2)}, u32[]{:S(2)}) async-start(bf16[16,32,128]{2,1,0:T(8,128)(2,1)} %get-tuple-element.85), calls=%async_computation.2 | async-start | bytes 262144 | tf_op jit(solution)/shard_map/all_to_all | solution.py:745
  47.3 0.7 copy-start.7
  56.5 0.7 copy-start.2
  62.6 11.9 %all-to-all-start.3 = ((bf16[16,32,128]{2,1,0:T(8,128)(2,1)}), bf16[16,32,128]{2,1,0:T(8,128)(2,1)S(1)}, u32[]{:S(2)}, u32[]{:S(2)}) async-start(bf16[16,32,128]{2,1,0:T(8,128)(2,1)} %get-tuple-element.91), calls=%async_computation.3 | async-start | bytes 262144 | tf_op jit(solution)/shard_map/all_to_all | solution.py:745
  69.5 18.8 %collective-permute-start.5 = (bf16[2,64,1024]{2,1,0:T(8,128)(2,1)}, bf16[2,64,1024]{2,1,0:T(8,128)(2,1)S(1)}, u32[]{:S(2)}, u32[]{:S(2)}) collective-permute-start(bf16[2,64,1024]{2,1,0:T(8,128)(2,1)} %get-tuple-element.107), channel_id=1, source_target_pairs={{0,1},{1,0},{2,3},{3,2},{4,5},{5,4},{6,7},{7,6},{8,9},{9,8},{10,11... | collective-permute-start | bytes 786440 | tf_op jit(solution)/shard_map/ppermute | solution.py:748
  76.4 12.8 %all-to-all-start.4 = ((bf16[16,64,128]{2,1,0:T(8,128)(2,1)}), bf16[16,64,128]{2,1,0:T(8,128)(2,1)S(1)}, u32[]{:S(2)}, u32[]{:S(2)}) async-start(bf16[16,64,128]{2,1,0:T(8,128)(2,1)} %get-tuple-element.97), calls=%async_computation.4 | async-start | bytes 524288 | tf_op jit(solution)/shard_map/all_to_all | solution.py:745
  80.6 8.6 %collective-permute-start.7 = (bf16[128,128]{1,0:T(8,128)(2,1)S(1)}, bf16[128,128]{1,0:T(8,128)(2,1)S(1)}, u32[]{:S(2)}, u32[]{:S(2)}) collective-permute-start(bf16[128,128]{1,0:T(8,128)(2,1)S(1)} %get-tuple-element.108), channel_id=1, source_target_pairs={{0,16},{1,17},{2,18},{3,19},{4,20},{5,21},{6,22},{7,23},{8,24},{9,... | collective-permute-start | bytes 98312 | tf_op jit(solution)/shard_map/ppermute | solution.py:748
  85.5 15.5 %collective-permute-start.4 = (bf16[2,128,1024]{2,1,0:T(8,128)(2,1)}, bf16[2,128,1024]{2,1,0:T(8,128)(2,1)S(1)}, u32[]{:S(2)}, u32[]{:S(2)}) collective-permute-start(bf16[2,128,1024]{2,1,0:T(8,128)(2,1)} %get-tuple-element.104), channel_id=1, source_target_pairs={{0,1},{1,0},{2,3},{3,2},{4,5},{5,4},{6,7},{7,6},{8,9},{9,8},{10,11... | collective-permute-start | bytes 1572872 | tf_op jit(solution)/shard_map/ppermute | solution.py:748
  86.4 1.9 %copy-start = (f32[2,64,1024]{2,1,0:T(8,128)S(1)}, f32[2,64,1024]{2,1,0:T(8,128)}, u32[]{:S(2)}) copy-start(f32[2,64,1024]{2,1,0:T(8,128)} %get-tuple-element.106) | copy-start | bytes 1572868
  88.4 12.7 %collective-permute-start.6 = (bf16[2,64,1024]{2,1,0:T(8,128)(2,1)S(1)}, bf16[2,64,1024]{2,1,0:T(8,128)(2,1)S(1)}, u32[]{:S(2)}, u32[]{:S(2)}) collective-permute-start(bf16[2,64,1024]{2,1,0:T(8,128)(2,1)S(1)} %add_convert_fusion), channel_id=1, source_target_pairs={{0,2},{1,3},{2,0},{3,1},{4,6},{5,7},{6,4},{7,5},{8,10},{9,11},{10,... | collective-permute-start | bytes 786440 | tf_op jit(solution)/shard_map/ppermute | solution.py:748
  90.5 15.1 %all-to-all-start.5 = ((bf16[16,48,128]{2,1,0:T(8,128)(2,1)}), bf16[16,48,128]{2,1,0:T(8,128)(2,1)S(1)}, u32[]{:S(2)}, u32[]{:S(2)}) async-start(bf16[16,48,128]{2,1,0:T(8,128)(2,1)} %shard_map.88), calls=%async_computation.5 | async-start | bytes 393216 | tf_op jit(solution)/shard_map/all_to_all | solution.py:745
  101.0 4.6 %copy-start.8 = (bf16[2,64,1024]{2,1,0:T(8,128)(2,1)}, bf16[2,64,1024]{2,1,0:T(8,128)(2,1)S(1)}, u32[]{:S(2)}) copy-start(bf16[2,64,1024]{2,1,0:T(8,128)(2,1)S(1)} %collective-permute-done.6.refs_6_) | copy-start | bytes 786436
  101.0 4.6 %copy-start.4 = (bf16[2,128,1024]{2,1,0:T(8,128)(2,1)}, bf16[2,128,1024]{2,1,0:T(8,128)(2,1)S(1)}, u32[]{:S(2)}) copy-start(bf16[2,128,1024]{2,1,0:T(8,128)(2,1)S(1)} %collective-permute-done.4.refs_4_) | copy-start | bytes 1572868
  105.6 0.7 copy-start.1

commit v2 on v1

--- a/solution.py
+++ b/solution.py
@@ -147,16 +147,7 @@
     return [first + i for i in range(1 << bit)]
 
 
-def prepare_kernel(me_ref, recv_ref, q_ref, kv_ref, block_ref, send_ref):
-    me = me_ref[0]
-    low16 = low_lanes(16)
-    for d in range(RING):
-        kv_ref[32 * d : 32 * d + 32, :] = recv_ref[d, 0:32, :]
-        packed = recv_ref[d, 32:48, :].astype(F32) * 0.125
-        q_ref[32 * d : 32 * d + 16, :] = jnp.where(low16, packed, 0.0).astype(BF16)
-        q_ref[32 * d + 16 : 32 * d + 32, :] = jnp.where(
-            low16, swap_halves(packed), 0.0
-        ).astype(BF16)
+def pool_stack(ref):
     for level in range(3, 8):
         rows = ROWS[level]
         step = min(rows, 256)
@@ -164,12 +155,16 @@
         for start in range(0, rows, step):
             source = slice(FIRST[level] + start, FIRST[level] + start + step)
             at = FIRST[level + 1] + start // 2
-            target = slice(at, at + step // 2)
-            q_ref[target, :] = dot(matrix, q_ref[source, :]).astype(BF16)
-            kv_ref[target, :] = dot(matrix, kv_ref[source, :]).astype(BF16)
+            ref[at : at + step // 2, :] = dot(matrix, ref[source, :]).astype(BF16)
     end = FIRST[8] + ROWS[8]
-    q_ref[end:STACK, :] = jnp.zeros((STACK - end, LANES), BF16)
-    kv_ref[end:STACK, :] = jnp.zeros((STACK - end, LANES), BF16)
+    ref[end:STACK, :] = jnp.zeros((STACK - end, LANES), BF16)
+
+
+def prepare_keys_kernel(me_ref, recv_ref, kv_ref, block_ref, send_ref):
+    me = me_ref[0]
+    for d in range(RING):
+        kv_ref[32 * d : 32 * d + 32, :] = recv_ref[d, 0:32, :]
+    pool_stack(kv_ref)
     block_ref[...] = kv_ref[FIRST[5] : FIRST[5] + B, :]
     send_ref[...] = jnp.zeros_like(send_ref)
     for level in range(6, 9):
@@ -177,6 +172,17 @@
         block = kv_ref[FIRST[level] : FIRST[level] + rows, :]
         for slot in sibling_slots(me, level):
             send_ref[slot, 0:rows, :] = block
+
+
+def prepare_queries_kernel(recv_ref, q_ref):
+    low16 = low_lanes(16)
+    for d in range(RING):
+        packed = recv_ref[d, 32:48, :].astype(F32) * 0.125
+        q_ref[32 * d : 32 * d + 16, :] = jnp.where(low16, packed, 0.0).astype(BF16)
+        q_ref[32 * d + 16 : 32 * d + 32, :] = jnp.where(
+            low16, swap_halves(packed), 0.0
+        ).astype(BF16)
+    pool_stack(q_ref)
 
 
 def heads_forward(pairs, bias):
@@ -214,14 +220,14 @@
 def own_forward_kernel(steps):
     pairs = [(q[...], k[...], v[...]) for q, k, v, _, _ in steps]
     for views, (att, lse) in zip(steps, heads_forward(pairs, 0.0)):
-        views[3][...] = att.astype(BF16)
+        views[3][...] = att
         views[4][...] = lse
 
 
 def core_forward_kernel(steps):
     pairs = [(q[...], kv[0], kv[1]) for q, kv, _, _ in steps]
     for views, (att, lse) in zip(steps, heads_forward(pairs, LN2)):
-        views[2][...] = att.astype(BF16)
+        views[2][...] = att
         views[3][...] = lse
 
 
@@ -235,7 +241,7 @@
 def ring_forward_kernel(steps):
     pairs = [(q[...],) + ring_pair(kva, kvb) for q, kva, kvb, _, _ in steps]
     for views, (att, lse) in zip(steps, heads_forward(pairs, 2.0 * LN2)):
-        views[3][...] = att.astype(BF16)
+        views[3][...] = att
         views[4][...] = lse
 
 
@@ -371,7 +377,7 @@
         e_up = jnp.exp(lse - high)
         e_own = jnp.exp(own_lse - high)
         den = e_up + e_own
-        att = (e_up * att + e_own * att_ref[...].astype(F32)) / den
+        att = (e_up * att + e_own * att_ref[...]) / den
         lse = high + jnp.log(den)
         yield
     attended = att.astype(BF16)
@@ -436,16 +442,28 @@
         send_ref[j, 16:32, :] = jnp.concatenate(parts + [tail], axis=0).astype(BF16)
 
 
-def level_backward(q, kv, least, grads, level):
-    rows = q.shape[0]
-    low = low_lanes(rows)
-    s = dot_nt(q, kv)
-    weight = jnp.exp(s + (level * LN2 - least[:, 0:1]))
-    cograd = jnp.where(low, 0.0, grads).astype(BF16)
-    slope = (weight * (dot_nt(cograd, kv) - grads[:, 0:1])).astype(BF16)
-    query_part = dot(slope, kv) * 0.125
-    other_part = dot_tn(slope, q) + dot_tn(weight.astype(BF16), cograd)
-    return query_part, other_part
+def levels_backward(items):
+    scores = [dot_nt(q, kv) for q, kv, _, _, _ in items]
+    cograds = [
+        jnp.where(low_lanes(q.shape[0]), 0.0, grads).astype(BF16)
+        for q, _, _, grads, _ in items
+    ]
+    through = [dot_nt(c, item[1]) for c, item in zip(cograds, items)]
+    weights = [
+        jnp.exp(s + (level * LN2 - least[:, 0:1]))
+        for s, (_, _, least, _, level) in zip(scores, items)
+    ]
+    slopes = [
+        (w * (t - item[3][:, 0:1])).astype(BF16)
+        for w, t, item in zip(weights, through, items)
+    ]
+    return [
+        (
+            dot(slope, item[1]) * 0.125,
+            dot_tn(slope, item[0]) + dot_tn(w.astype(BF16), c),
+        )
+        for slope, w, c, item in zip(slopes, weights, cograds, items)
+    ]
 
 
 def unpack_and_fold(recv_ref, r_ref, g_ref, last):
@@ -479,12 +497,16 @@
     unpack_and_fold(recv_ref, r_ref, g_ref, 8)
     send_ref[...] = jnp.zeros_like(send_ref)
     running = None
-    for level in (8, 7, 6, 5):
+    levels = (8, 7, 6, 5)
+    spans = [slice(FIRST[level], FIRST[level] + ROWS[level]) for level in levels]
+    results = levels_backward(
+        [
+            (q_ref[at, :], sibling_ref[level - 5], r_ref[at, :], g_ref[at, :], level)
+            for level, at in zip(levels, spans)
+        ]
+    )
+    for level, (query_part, other_part) in zip(levels, results):
         rows = ROWS[level]
-        at = slice(FIRST[level], FIRST[level] + rows)
-        query_part, other_part = level_backward(
-            q_ref[at, :], sibling_ref[level - 5], r_ref[at, :], g_ref[at, :], level
-        )
         other_part = other_part.astype(BF16)
         if level == 5:
             beside_ref[...] = other_part
@@ -506,16 +528,19 @@
         blocks = ROWS[level] // B
         query_parts = [None] * blocks
         other_parts = [None] * blocks
-        for block in range(blocks):
-            at = FIRST[level] + B * block
-            beside = FIRST[level] + B * (block ^ 1)
-            query_part, other_part = level_backward(
-                q_ref[at : at + B, :],
-                kv_ref[beside : beside + B, :],
-                r_ref[at : at + B, :],
-                g_ref[at : at + B, :],
-                level,
-            )
+        results = levels_backward(
+            [
+                (
+                    q_ref[FIRST[level] + B * i : FIRST[level] + B * i + B, :],
+                    kv_ref[FIRST[level] + B * (i ^ 1) : FIRST[level] + B * (i ^ 1) + B, :],
+                    r_ref[FIRST[level] + B * i : FIRST[level] + B * i + B, :],
+                    g_ref[FIRST[level] + B * i : FIRST[level] + B * i + B, :],
+                    level,
+                )
+                for i in range(blocks)
+            ]
+        )
+        for block, (query_part, other_part) in enumerate(results):
             query_parts[block] = query_part
             other_parts[block ^ 1] = other_part
         for block in range(blocks):
@@ -768,7 +793,7 @@
     full = ((rows, width), F32)
     att0, lse0 = over_pairs(
         own_forward_kernel,
-        [((rows, width), BF16), full],
+        [full, full],
         [Tall(rows)] * 2,
         (q, k, v),
         [Tall(rows)] * 3,
@@ -778,12 +803,14 @@
         moved=1e7,
     )
     recv1, att0 = lax.optimization_barrier((recv1, att0))
-    qh, kvh, block, sendx = call(
-        prepare_kernel,
-        [((STACK, LANES), BF16)] * 2 + [((B, LANES), BF16), ((RING, 64, LANES), BF16)],
+    kvh, block, sendx = call(
+        prepare_keys_kernel,
+        [((STACK, LANES), BF16), ((B, LANES), BF16), ((RING, 64, LANES), BF16)],
         (me, recv1),
         smem_first=True,
     )
+    sendx, recv1 = lax.optimization_barrier((sendx, recv1))
+    (qh,) = call(prepare_queries_kernel, [((STACK, LANES), BF16)], (recv1,))
     sendx, kv2 = lax.optimization_barrier((sendx, kv2))
     beside = swapped(block, RING)
     kv2a = swapped(kv2, 2)
@@ -792,7 +819,7 @@
     half = (B, width)
     att1, lse1 = over_pairs(
         core_forward_kernel,
-        [(half, BF16), (half, F32)],
+        [(half, F32), (half, F32)],
         [Tall(B)] * 2,
         (q1, kv1s),
         [Tall(B), TwoTall(B)],
@@ -814,7 +841,7 @@
     recv2 = exchange(send2, rings)
     att2, lse2 = over_pairs(
         ring_forward_kernel,
-        [(quarter, BF16), (quarter, F32)],
+        [(quarter, F32), (quarter, F32)],
         [Tall(64)] * 2,
         (q2_later, kv2a, kv2b),
         [Tall(64), TwoTall(64), TwoTall(64)],

time: 110 us -> 111 us (level)
    pallas_call x6 -> x7, Pallas kernels: 9.65 us -> 9.65 us  [call(): pl.pallas_call(kernel, out_shape=[jax.ShapeDtypeStruct(s, d) for s, d in...]
where the time goes in v2:
time: 111 us; the launch traced here: 110 us
  Pallas kernels  43.6 us (39%)
  starting transfers between devices  40.3 us (36%)
  waiting for transfers between devices  22.6 us (20%)
  local copies, waits for them, and re-layouts  2.83 us (3%)
    all_to_all x6, starting transfers between devices, exchange(): return lax.all_to_all(x, 'seq', 0, 0, axis_index_groups=groups, tiled=True)  35.1 us
    pallas_call x9, Pallas kernels, over_pairs(): pl.pallas_call(body, grid=(PAIRS // step,), out_shape=[jax.ShapeDtypeStru...  33.9 us
    all_to_all x6, waiting for transfers between devices, exchange(): return lax.all_to_all(x, 'seq', 0, 0, axis_index_groups=groups, tiled=True)  22.6 us
    pallas_call x7, Pallas kernels, call(): pl.pallas_call(kernel, out_shape=[jax.ShapeDtypeStruct(s, d) for s, d in...  9.65 us
    ppermute x8, starting transfers between devices, swapped(): return lax.ppermute(x, 'seq', pairs_of(mask, size))  5.19 us
    unnamed x18, local copies, waits for them, and re-layouts  2.83 us
  transfers between devices with their start and end apart: 14, of which 6 were waited for; matrix products, arithmetic and copies ran while one was open for 0% of the time, Pallas kernels for 29%

profile of v2, /device:TPU:1, one launch (start us, length us, event | category | flops | bytes accessed | tf_op | source)
XLA Modules:
  0.0 110.2 jit_solution(4552309037583413480)
XLA Ops:
  0.6 2.9 %shard_map.75 = (bf16[128,1024]{1,0:T(8,128)(2,1)}, bf16[2,128,1024]{2,1,0:T(8,128)(2,1)}, bf16[64,1024]{1,0:T(8,128)(2,1)}, bf16[2,64,1024]{2,1,0:T(8,128)(2,1)}, bf16[16,48,128]{2,1,0:T(8,128)(2,1)}) custom-call(bf16[256,1024]{1,0:T(8,128)(2,1)} %refs_0_.5, bf16[256,1024]{1,0:T(8,128)(2,1)} %refs_1_.5, bf16[256,1024]{1,0:T(8,128)(2,1)} %refs_2_.5), custom_call_target="tpu_custom_call" | custom-call | flops 1000000000 | bytes 5000000 | tf_op jit(solution)/shard_map/pallas_call | solution.py:744
  3.5 10.0 %all-to-all-start = ((bf16[16,48,128]{2,1,0:T(8,128)(2,1)}), bf16[16,48,128]{2,1,0:T(8,128)(2,1)S(1)}, u32[]{:S(2)}, u32[]{:S(2)}) async-start(bf16[16,48,128]{2,1,0:T(8,128)(2,1)} %get-tuple-element.61), calls=%async_computation | async-start | bytes 393216 | tf_op jit(solution)/shard_map/all_to_all | solution.py:770
  13.7 4.0 %shard_map.76 = (f32[256,1024]{1,0:T(8,128)}, f32[256,1024]{1,0:T(8,128)}) custom-call(bf16[256,1024]{1,0:T(8,128)(2,1)} %refs_0_.5, bf16[256,1024]{1,0:T(8,128)(2,1)} %refs_1_.5, bf16[256,1024]{1,0:T(8,128)(2,1)} %refs_2_.5), custom_call_target="tpu_custom_call" | custom-call | flops 6000000000 | bytes 10000000 | tf_op jit(solution)/shard_map/pallas_call | solution.py:744
  17.7 6.1 %all-to-all-done.recv_ref = bf16[16,48,128]{2,1,0:T(8,128)(2,1)S(1)} async-done(((bf16[16,48,128]{2,1,0:T(8,128)(2,1)}), bf16[16,48,128]{2,1,0:T(8,128)(2,1)S(1)}, u32[]{:S(2)}, u32[]{:S(2)}) %all-to-all-start) | async-done | bytes 196640 | tf_op jit(solution)/shard_map/all_to_all | solution.py:770
  23.8 1.5 %shard_map.77 = (bf16[1024,128]{1,0:T(8,128)(2,1)S(1)}, bf16[128,128]{1,0:T(8,128)(2,1)S(1)}, bf16[16,64,128]{2,1,0:T(8,128)(2,1)}) custom-call(s32[1]{0:T(128)} %bitcast.me_ref, bf16[16,48,128]{2,1,0:T(8,128)(2,1)S(1)} %all-to-all-done.recv_ref), custom_call_target="tpu_custom_call" | custom-call | flops 100000000 | bytes 2000000 | tf_op jit(solution)/shard_map/pallas_call | solution.py:102
  25.3 6.8 %all-to-all-start.1 = ((bf16[16,64,128]{2,1,0:T(8,128)(2,1)}), bf16[16,64,128]{2,1,0:T(8,128)(2,1)S(1)}, u32[]{:S(2)}, u32[]{:S(2)}) async-start(bf16[16,64,128]{2,1,0:T(8,128)(2,1)} %get-tuple-element.69), calls=%async_computation.1 | async-start | bytes 524288 | tf_op jit(solution)/shard_map/all_to_all | solution.py:770
  32.1 1.4 %collective-permute-start.1 = (bf16[128,128]{1,0:T(8,128)(2,1)S(1)}, bf16[128,128]{1,0:T(8,128)(2,1)S(1)}, u32[]{:S(2)}, u32[]{:S(2)}) collective-permute-start(bf16[128,128]{1,0:T(8,128)(2,1)S(1)} %get-tuple-element.75), channel_id=1, source_target_pairs={{0,16},{1,17},{2,18},{3,19},{4,20},{5,21},{6,22},{7,23},{8,24},{9,... | collective-permute-start | bytes 98312 | tf_op jit(solution)/shard_map/ppermute | solution.py:773
  33.4 0.8 shard_map.79.q_ref
  34.2 1.1 collective-permute-start.3
  35.3 1.1 %shard_map.80 = (f32[512,128]{1,0:T(8,128)S(1)}, f32[512,128]{1,0:T(8,128)S(1)}) custom-call(bf16[1024,128]{1,0:T(8,128)(2,1)S(1)} %shard_map.79.q_ref, bf16[1024,128]{1,0:T(8,128)(2,1)S(1)} %get-tuple-element.78.kv_ref), custom_call_target="tpu_custom_call" | custom-call | flops 1000000000 | bytes 2000000 | tf_op jit(solution)/shard_map/pallas_call | solution.py:102
  36.5 0.8 copy-done.3
  37.3 2.9 %shard_map.78 = (f32[128,1024]{1,0:T(8,128)}, f32[128,1024]{1,0:T(8,128)}) custom-call(bf16[128,1024]{1,0:T(8,128)(2,1)} %get-tuple-element.101.refs_0_, bf16[2,128,1024]{2,1,0:T(8,128)(2,1)} %copy-done.3), custom_call_target="tpu_custom_call" | custom-call | flops 2000000000 | bytes 5000000 | tf_op jit(solution)/shard_map/pallas_call | solution.py:744
  40.3 1.9 %shard_map.81 = (bf16[16,32,128]{2,1,0:T(8,128)(2,1)}, bf16[4,128,128]{2,1,0:T(8,128)(2,1)S(1)}) custom-call(s32[1]{0:T(128)} %bitcast.me_ref, bf16[128,128]{1,0:T(8,128)(2,1)S(1)} %collective-permute-done.1.beside_ref, bf16[16,64,128]{2,1,0:T(8,128)(2,1)S(1)} %all-to-all-done.1.recv_ref, bf16[1024,128]{1,0:T(8,128)(2,1)S(1)} %shard_map.79.q_ref, ...), custom_call_target="tpu_custom_call" | custom-call | flops 100000000 | bytes 2000000 | tf_op jit(solution)/shard_map/pallas_call | solution.py:102
  42.2 5.0 %all-to-all-start.2 = ((bf16[16,32,128]{2,1,0:T(8,128)(2,1)}), bf16[16,32,128]{2,1,0:T(8,128)(2,1)S(1)}, u32[]{:S(2)}, u32[]{:S(2)}) async-start(bf16[16,32,128]{2,1,0:T(8,128)(2,1)} %get-tuple-element.87), calls=%async_computation.2 | async-start | bytes 262144 | tf_op jit(solution)/shard_map/all_to_all | solution.py:770
  48.0 2.7 %shard_map.82 = (f32[64,1024]{1,0:T(8,128)}, f32[64,1024]{1,0:T(8,128)}) custom-call(bf16[64,1024]{1,0:T(8,128)(2,1)} %get-tuple-element.83.refs_0_, bf16[2,64,1024]{2,1,0:T(8,128)(2,1)} %copy-done.5, bf16[2,64,1024]{2,1,0:T(8,128)(2,1)} %copy-done.7), custom_call_target="tpu_custom_call" | custom-call | flops 2000000000 | bytes 5000000 | tf_op jit(solution)/shard_map/pallas_call | solution.py:744
  50.7 5.8 %all-to-all-done.2.refs_6_ = bf16[16,32,128]{2,1,0:T(8,128)(2,1)S(1)} async-done(((bf16[16,32,128]{2,1,0:T(8,128)(2,1)}), bf16[16,32,128]{2,1,0:T(8,128)(2,1)S(1)}, u32[]{:S(2)}, u32[]{:S(2)}) %all-to-all-start.2) | async-done | bytes 131104 | tf_op jit(solution)/shard_map/all_to_all | solution.py:770
  57.1 5.5 %shard_map.83 = (bf16[256,1024]{1,0:T(8,128)(2,1)}, f32[256,1024]{1,0:T(8,128)}, f32[128,1024]{1,0:T(8,128)}, bf16[128,1024]{1,0:T(8,128)(2,1)}, f32[64,1024]{1,...) custom-call(f32[256,1024]{1,0:T(8,128)} %get-tuple-element.63.refs_0_, ...), custom_call_target="tpu_custom_call" | custom-call | flops 1000000000 | bytes 5000000 | tf_op jit(solution)/shard_map/pallas_call | solution.py:744
  62.7 3.4 %all-to-all-start.3 = ((bf16[16,32,128]{2,1,0:T(8,128)(2,1)}), bf16[16,32,128]{2,1,0:T(8,128)(2,1)S(1)}, u32[]{:S(2)}, u32[]{:S(2)}) async-start(bf16[16,32,128]{2,1,0:T(8,128)(2,1)} %get-tuple-element.93), calls=%async_computation.3 | async-start | bytes 262144 | tf_op jit(solution)/shard_map/all_to_all | solution.py:770
  66.1 3.5 %shard_map.85 = (bf16[64,1024]{1,0:T(8,128)(2,1)}, f32[2,64,1024]{2,1,0:T(8,128)}, bf16[2,64,1024]{2,1,0:T(8,128)(2,1)}) custom-call(bf16[64,1024]{1,0:T(8,128)(2,1)} %get-tuple-element.83.refs_0_, bf16[2,64,1024]{2,1,0:T(8,128)(2,1)} %copy-done.5, bf16[2,64,1024]{2,1,0:T(8,128)(2,1)} %copy-done.7, f32[64,1024]{1,0:T(8,128)} %get-tuple-element.94.refs_3_, ...), custom_call_target="tpu_custom_call" | custom-call | flops 3000000000 | bytes 5000000 | tf_op jit(solution)/shard_map/pallas_call | solution.py:744
  69.6 5.0 %all-to-all-done.3.recv_ref = bf16[16,32,128]{2,1,0:T(8,128)(2,1)S(1)} async-done(((bf16[16,32,128]{2,1,0:T(8,128)(2,1)}), bf16[16,32,128]{2,1,0:T(8,128)(2,1)S(1)}, u32[]{:S(2)}, u32[]{:S(2)}) %all-to-all-start.3) | async-done | bytes 131104 | tf_op jit(solution)/shard_map/all_to_all | solution.py:770
  74.6 1.6 %shard_map.86 = (f32[128,128]{1,0:T(8,128)S(1)}, bf16[128,128]{1,0:T(8,128)(2,1)S(1)}, bf16[16,64,128]{2,1,0:T(8,128)(2,1)}) custom-call(s32[1]{0:T(128)} %bitcast.me_ref, bf16[16,32,128]{2,1,0:T(8,128)(2,1)S(1)} %all-to-all-done.3.recv_ref, bf16[1024,128]{1,0:T(8,128)(2,1)S(1)} %shard_map.79.q_ref, bf16[4,128,128]{2,1,0:T(8,128)(2,1)S(1)} %get-tuple-element.98.sibling_ref), custom_call_target="tpu_custom_call" | custom-call | flops 100000000 | bytes 2000000 | tf_op jit(solution)/shard_map/pallas_call | solution.py:102
  76.2 5.2 %all-to-all-start.4 = ((bf16[16,64,128]{2,1,0:T(8,128)(2,1)}), bf16[16,64,128]{2,1,0:T(8,128)(2,1)S(1)}, u32[]{:S(2)}, u32[]{:S(2)}) async-start(bf16[16,64,128]{2,1,0:T(8,128)(2,1)} %get-tuple-element.99), calls=%async_computation.4 | async-start | bytes 524288 | tf_op jit(solution)/shard_map/all_to_all | solution.py:770
  81.4 1.4 %collective-permute-start.7 = (bf16[128,128]{1,0:T(8,128)(2,1)S(1)}, bf16[128,128]{1,0:T(8,128)(2,1)S(1)}, u32[]{:S(2)}, u32[]{:S(2)}) collective-permute-start(bf16[128,128]{1,0:T(8,128)(2,1)S(1)} %get-tuple-element.110), channel_id=1, source_target_pairs={{0,16},{1,17},{2,18},{3,19},{4,20},{5,21},{6,22},{7,23},{8,24},{9,... | collective-permute-start | bytes 98312 | tf_op jit(solution)/shard_map/ppermute | solution.py:773
  82.8 3.6 %shard_map.87 = (bf16[128,1024]{1,0:T(8,128)(2,1)}, bf16[2,128,1024]{2,1,0:T(8,128)(2,1)}) custom-call(bf16[128,1024]{1,0:T(8,128)(2,1)} %get-tuple-element.101.refs_0_, bf16[2,128,1024]{2,1,0:T(8,128)(2,1)} %copy-done.3, f32[128,1024]{1,0:T(8,128)} %get-tuple-element.102.refs_2_, bf16[128,1024]{1,0:T(8,128)(2,1)} %get-tuple-element.103.refs_3_), custom_call_target="tpu_custom_call" | custom-call | flops 3000000000 | bytes 5000000 | tf_op jit(solution)/shard_map/pallas_call | solution.py:744
  86.3 0.8 collective-permute-start.4
  87.1 1.4 %shard_map.88 = (f32[512,128]{1,0:T(8,128)S(1)}, f32[512,128]{1,0:T(8,128)S(1)}) custom-call(bf16[1024,128]{1,0:T(8,128)(2,1)S(1)} %shard_map.79.q_ref, bf16[1024,128]{1,0:T(8,128)(2,1)S(1)} %get-tuple-element.78.kv_ref, bf16[16,32,128]{2,1,0:T(8,128)(2,1)S(1)} %all-to-all-done.3.recv_ref, f32[128,128]{1,0:T(8,128)S(1)} %get-tuple-element.112.q5_ref), custom_call_target="tpu_custom_call" | custom-call | flops 2000000000 | bytes 2000000 | tf_op jit(solution)/shard_map/pallas_call | solution.py:102
  89.0 1.0 all-to-all-done.4.recv_ref
  89.9 1.3 %shard_map.89 = bf16[16,48,128]{2,1,0:T(8,128)(2,1)} custom-call(s32[1]{0:T(128)} %bitcast.me_ref, bf16[128,128]{1,0:T(8,128)(2,1)S(1)} %collective-permute-done.7.beside_ref, bf16[16,64,128]{2,1,0:T(8,128)(2,1)S(1)} %all-to-all-done.4.recv_ref, f32[512,128]{1,0:T(8,128)S(1)} %get-tuple-element.113.query_ref, f32[512,128]{1,0:T(8,128)S(1)} %get-tuple-element.114.other_ref), custom_call_target="tpu_custom_call" | custom-call | flops 100000000 | bytes 2000000 | tf_op jit(solution)/shard_map/pallas_call | solution.py:102
  91.3 4.7 %all-to-all-start.5 = ((bf16[16,48,128]{2,1,0:T(8,128)(2,1)}), bf16[16,48,128]{2,1,0:T(8,128)(2,1)S(1)}, u32[]{:S(2)}, u32[]{:S(2)}) async-start(bf16[16,48,128]{2,1,0:T(8,128)(2,1)} %shard_map.89), calls=%async_computation.5 | async-start | bytes 393216 | tf_op jit(solution)/shard_map/all_to_all | solution.py:770
  96.0 5.8 %shard_map.84 = (bf16[256,1024]{1,0:T(8,128)(2,1)}, bf16[256,1024]{1,0:T(8,128)(2,1)}, bf16[256,1024]{1,0:T(8,128)(2,1)}) custom-call(bf16[256,1024]{1,0:T(8,128)(2,1)} %refs_0_.5, bf16[256,1024]{1,0:T(8,128)(2,1)} %refs_1_.5, bf16[256,1024]{1,0:T(8,128)(2,1)} %refs_2_.5, bf16[256,1024]{1,0:T(8,128)(2,1)} %refs_3_.1, f32[256,1024]{1,0:T(8,128)} %get-tuple-element.89.refs_4_), custom_call_target="tpu_custom_call" | custom-call | flops 8999999488 | bytes 10000000 | tf_op jit(solution)/shard_map/pallas_call | solution.py:744
  101.8 4.6 %all-to-all-done.5.refs_7_ = bf16[16,48,128]{2,1,0:T(8,128)(2,1)S(1)} async-done(((bf16[16,48,128]{2,1,0:T(8,128)(2,1)}), bf16[16,48,128]{2,1,0:T(8,128)(2,1)S(1)}, u32[]{:S(2)}, u32[]{:S(2)}) %all-to-all-start.5) | async-done | bytes 196640 | tf_op jit(solution)/shard_map/all_to_all | solution.py:770
  107.1 3.1 %shard_map.90 = (bf16[256,1024]{1,0:T(8,128)(2,1)}, bf16[256,1024]{1,0:T(8,128)(2,1)}, bf16[256,1024]{1,0:T(8,128)(2,1)}) custom-call(bf16[256,1024]{1,0:T(8,128)(2,1)} %get-tuple-element.90.refs_0_, bf16[256,1024]{1,0:T(8,128)(2,1)} %get-tuple-element.91.refs_1_, bf16[256,1024]{1,0:T(8,128)(2,1)} %get-tuple-element.92.refs_2_, ...), custom_call_target="tpu_custom_call" | custom-call | flops 1000000000 | bytes 5000000 | tf_op jit(solution)/shard_map/pallas_call | solution.py:744
  (31 shorter events, 2.8 us)
Async XLA Ops:
  3.5 20.3 %all-to-all-start = ((bf16[16,48,128]{2,1,0:T(8,128)(2,1)}), bf16[16,48,128]{2,1,0:T(8,128)(2,1)S(1)}, u32[]{:S(2)}, u32[]{:S(2)}) async-start(bf16[16,48,128]{2,1,0:T(8,128)(2,1)} %get-tuple-element.61), calls=%async_computation | async-start | bytes 393216 | tf_op jit(solution)/shard_map/all_to_all | solution.py:770
  13.5 23.0 %collective-permute-start = (bf16[2,128,1024]{2,1,0:T(8,128)(2,1)}, bf16[2,128,1024]{2,1,0:T(8,128)(2,1)S(1)}, u32[]{:S(2)}, u32[]{:S(2)}) collective-permute-start(bf16[2,128,1024]{2,1,0:T(8,128)(2,1)} %get-tuple-element.71), channel_id=1, source_target_pairs={{0,1},{1,0},{2,3},{3,2},{4,5},{5,4},{6,7},{7,6},{8,9},{9,8},{10,11... | collective-permute-start | bytes 1572872 | tf_op jit(solution)/shard_map/ppermute | solution.py:773
  17.7 7.6 %copy-start.6 = (bf16[2,64,1024]{2,1,0:T(8,128)(2,1)S(1)}, bf16[2,64,1024]{2,1,0:T(8,128)(2,1)}, u32[]{:S(2)}) copy-start(bf16[2,64,1024]{2,1,0:T(8,128)(2,1)} %get-tuple-element.84) | copy-start | bytes 786436
  25.3 8.9 %collective-permute-start.2 = (bf16[2,64,1024]{2,1,0:T(8,128)(2,1)S(1)}, bf16[2,64,1024]{2,1,0:T(8,128)(2,1)S(1)}, u32[]{:S(2)}, u32[]{:S(2)}) collective-permute-start(bf16[2,64,1024]{2,1,0:T(8,128)(2,1)S(1)} %copy-done.6), channel_id=1, source_target_pairs={{0,2},{1,3},{2,0},{3,1},{4,6},{5,7},{6,4},{7,5},{8,10},{9,11},{10,... | collective-permute-start | bytes 786440 | tf_op jit(solution)/shard_map/ppermute | solution.py:773
  25.3 15.0 %all-to-all-start.1 = ((bf16[16,64,128]{2,1,0:T(8,128)(2,1)}), bf16[16,64,128]{2,1,0:T(8,128)(2,1)S(1)}, u32[]{:S(2)}, u32[]{:S(2)}) async-start(bf16[16,64,128]{2,1,0:T(8,128)(2,1)} %get-tuple-element.69), calls=%async_computation.1 | async-start | bytes 524288 | tf_op jit(solution)/shard_map/all_to_all | solution.py:770
  32.1 8.3 %collective-permute-start.1 = (bf16[128,128]{1,0:T(8,128)(2,1)S(1)}, bf16[128,128]{1,0:T(8,128)(2,1)S(1)}, u32[]{:S(2)}, u32[]{:S(2)}) collective-permute-start(bf16[128,128]{1,0:T(8,128)(2,1)S(1)} %get-tuple-element.75), channel_id=1, source_target_pairs={{0,16},{1,17},{2,18},{3,19},{4,20},{5,21},{6,22},{7,23},{8,24},{9,... | collective-permute-start | bytes 98312 | tf_op jit(solution)/shard_map/ppermute | solution.py:773
  34.2 2.2 %copy-start.5 = (bf16[2,64,1024]{2,1,0:T(8,128)(2,1)}, bf16[2,64,1024]{2,1,0:T(8,128)(2,1)S(1)}, u32[]{:S(2)}) copy-start(bf16[2,64,1024]{2,1,0:T(8,128)(2,1)S(1)} %collective-permute-done.2.refs_1_) | copy-start | bytes 786436
  34.2 13.1 %collective-permute-start.3 = (bf16[2,64,1024]{2,1,0:T(8,128)(2,1)S(1)}, bf16[2,64,1024]{2,1,0:T(8,128)(2,1)S(1)}, u32[]{:S(2)}, u32[]{:S(2)}) collective-permute-start(bf16[2,64,1024]{2,1,0:T(8,128)(2,1)S(1)} %collective-permute-done.2.refs_1_), channel_id=1, source_target_pairs={{0,1},{1,0},{2,3},{3,2},{4,5},{5,4},{6,7},{7,6},{8,9},{9,8},{10,11... | collective-permute-start | bytes 786440 | tf_op jit(solution)/shard_map/ppermute | solution.py:773
  36.5 0.8 copy-start.3
  42.2 14.2 %all-to-all-start.2 = ((bf16[16,32,128]{2,1,0:T(8,128)(2,1)}), bf16[16,32,128]{2,1,0:T(8,128)(2,1)S(1)}, u32[]{:S(2)}, u32[]{:S(2)}) async-start(bf16[16,32,128]{2,1,0:T(8,128)(2,1)} %get-tuple-element.87), calls=%async_computation.2 | async-start | bytes 262144 | tf_op jit(solution)/shard_map/all_to_all | solution.py:770
  47.3 0.7 copy-start.7
  56.5 0.7 copy-start
  62.7 11.9 %all-to-all-start.3 = ((bf16[16,32,128]{2,1,0:T(8,128)(2,1)}), bf16[16,32,128]{2,1,0:T(8,128)(2,1)S(1)}, u32[]{:S(2)}, u32[]{:S(2)}) async-start(bf16[16,32,128]{2,1,0:T(8,128)(2,1)} %get-tuple-element.93), calls=%async_computation.3 | async-start | bytes 262144 | tf_op jit(solution)/shard_map/all_to_all | solution.py:770
  69.6 18.9 %collective-permute-start.5 = (bf16[2,64,1024]{2,1,0:T(8,128)(2,1)}, bf16[2,64,1024]{2,1,0:T(8,128)(2,1)S(1)}, u32[]{:S(2)}, u32[]{:S(2)}) collective-permute-start(bf16[2,64,1024]{2,1,0:T(8,128)(2,1)} %get-tuple-element.109), channel_id=1, source_target_pairs={{0,1},{1,0},{2,3},{3,2},{4,5},{5,4},{6,7},{7,6},{8,9},{9,8},{10,11... | collective-permute-start | bytes 786440 | tf_op jit(solution)/shard_map/ppermute | solution.py:773
  76.2 13.7 %all-to-all-start.4 = ((bf16[16,64,128]{2,1,0:T(8,128)(2,1)}), bf16[16,64,128]{2,1,0:T(8,128)(2,1)S(1)}, u32[]{:S(2)}, u32[]{:S(2)}) async-start(bf16[16,64,128]{2,1,0:T(8,128)(2,1)} %get-tuple-element.99), calls=%async_computation.4 | async-start | bytes 524288 | tf_op jit(solution)/shard_map/all_to_all | solution.py:770
  81.4 8.6 %collective-permute-start.7 = (bf16[128,128]{1,0:T(8,128)(2,1)S(1)}, bf16[128,128]{1,0:T(8,128)(2,1)S(1)}, u32[]{:S(2)}, u32[]{:S(2)}) collective-permute-start(bf16[128,128]{1,0:T(8,128)(2,1)S(1)} %get-tuple-element.110), channel_id=1, source_target_pairs={{0,16},{1,17},{2,18},{3,19},{4,20},{5,21},{6,22},{7,23},{8,24},{9,... | collective-permute-start | bytes 98312 | tf_op jit(solution)/shard_map/ppermute | solution.py:773
  86.3 15.5 %collective-permute-start.4 = (bf16[2,128,1024]{2,1,0:T(8,128)(2,1)}, bf16[2,128,1024]{2,1,0:T(8,128)(2,1)S(1)}, u32[]{:S(2)}, u32[]{:S(2)}) collective-permute-start(bf16[2,128,1024]{2,1,0:T(8,128)(2,1)} %get-tuple-element.106), channel_id=1, source_target_pairs={{0,1},{1,0},{2,3},{3,2},{4,5},{5,4},{6,7},{7,6},{8,9},{9,8},{10,11... | collective-permute-start | bytes 1572872 | tf_op jit(solution)/shard_map/ppermute | solution.py:773
  87.1 1.4 %copy-start.1 = (f32[2,64,1024]{2,1,0:T(8,128)S(1)}, f32[2,64,1024]{2,1,0:T(8,128)}, u32[]{:S(2)}) copy-start(f32[2,64,1024]{2,1,0:T(8,128)} %get-tuple-element.108) | copy-start | bytes 1572868
  88.6 13.2 %collective-permute-start.6 = (bf16[2,64,1024]{2,1,0:T(8,128)(2,1)S(1)}, bf16[2,64,1024]{2,1,0:T(8,128)(2,1)S(1)}, u32[]{:S(2)}, u32[]{:S(2)}) collective-permute-start(bf16[2,64,1024]{2,1,0:T(8,128)(2,1)S(1)} %add_convert_fusion), channel_id=1, source_target_pairs={{0,2},{1,3},{2,0},{3,1},{4,6},{5,7},{6,4},{7,5},{8,10},{9,11},{10,... | collective-permute-start | bytes 786440 | tf_op jit(solution)/shard_map/ppermute | solution.py:773
  91.3 15.1 %all-to-all-start.5 = ((bf16[16,48,128]{2,1,0:T(8,128)(2,1)}), bf16[16,48,128]{2,1,0:T(8,128)(2,1)S(1)}, u32[]{:S(2)}, u32[]{:S(2)}) async-start(bf16[16,48,128]{2,1,0:T(8,128)(2,1)} %shard_map.89), calls=%async_computation.5 | async-start | bytes 393216 | tf_op jit(solution)/shard_map/all_to_all | solution.py:770
  101.8 4.6 %copy-start.8 = (bf16[2,64,1024]{2,1,0:T(8,128)(2,1)}, bf16[2,64,1024]{2,1,0:T(8,128)(2,1)S(1)}, u32[]{:S(2)}) copy-start(bf16[2,64,1024]{2,1,0:T(8,128)(2,1)S(1)} %collective-permute-done.6.refs_6_) | copy-start | bytes 786436
  101.8 4.6 %copy-start.4 = (bf16[2,128,1024]{2,1,0:T(8,128)(2,1)}, bf16[2,128,1024]{2,1,0:T(8,128)(2,1)S(1)}, u32[]{:S(2)}) copy-start(bf16[2,128,1024]{2,1,0:T(8,128)(2,1)S(1)} %collective-permute-done.4.refs_4_) | copy-start | bytes 1572868
  106.4 0.7 copy-start.2
